TPU v7x, 256 devices: a whole 4x4x8 slice. The times are simulated.
256 devices in a mesh: depth: 16 (over x_lo, y, core), dp: 16 (over x_hi, z).
Axes of the slice: x: 4 (x_hi: 2, x_lo: 2; x = x_hi * 2 + x_lo), y: 4, z: 8, core: 2. Of those that a mesh axis runs over, the one named last changes fastest.
Arguments:
- token_ids: int32 [2048], P('dp'), may hold values from 0 to 20479
- embedding: bfloat16 [20480, 512], P('depth'), may hold values from -6 to 6
- w_up: bfloat16 [32, 512, 2048], P('depth'), may hold values from -0.25 to 0.25
- w_down: bfloat16 [32, 2048, 512], P('depth'), may hold values from -0.125 to 0.125
- cotangent: bfloat16 [2048, 512], P('dp'), may hold values from -0.119628906 to 0.119628906
Outputs:
- grad_up: float32 [32, 512, 2048], P('depth', 'dp')
- grad_down: float32 [32, 2048, 512], P('depth', 'dp')
All inputs are finite; a program needn't handle non-finite values.
Results may differ from a plain program's by a relative error of at most 0.03.
Values may be sent and summed in bfloat16 or wider, within the bound.
A program may use at most 64 MiB of HBM per device.

v0:
```python
import jax
import jax.numpy as jnp
from jax import lax
from jax.sharding import PartitionSpec as P

RELAX = 3


EPSILON = 1e-06
GAMMA = 0.05


def shifted(block, axis, distance):
    devices = range(lax.axis_size(axis))
    route = [(i - distance, i) for i in devices if i - distance in devices]
    return lax.ppermute(block, axis, route)


def layer_forward(state, weight_up, weight_down):
    scale = lax.rsqrt(jnp.mean(state * state, axis=-1, keepdims=True) + EPSILON)
    normed = (state * scale).astype(jnp.bfloat16)
    before = jnp.dot(normed, weight_up, preferred_element_type=jnp.float32)
    hidden = jax.nn.silu(before).astype(jnp.bfloat16)
    output = state + jnp.dot(hidden, weight_down, preferred_element_type=jnp.float32)
    return (output, (scale, normed, before, hidden))


def layer_adjoint(state, saved, adjoint, weight_up, weight_down):
    scale, normed, before, hidden = saved
    adjoint_low = adjoint.astype(jnp.bfloat16)
    toward_hidden = lax.dot_general(
        adjoint_low, weight_down, (((1,), (1,)), ((), ())), preferred_element_type=jnp.float32
    )
    sigma = jax.nn.sigmoid(before)
    delta = (toward_hidden * sigma * (1.0 + before * (1.0 - sigma))).astype(jnp.bfloat16)
    toward_normed = lax.dot_general(
        delta, weight_up, (((1,), (1,)), ((), ())), preferred_element_type=jnp.float32
    )
    unit = state * scale
    inner = jnp.mean(toward_normed * unit, axis=-1, keepdims=True)
    return (adjoint + scale * (toward_normed - unit * inner), adjoint_low, delta)


def coarse_matrix(weight_up, weight_down):
    total = jnp.dot(weight_up[0], weight_down[0], preferred_element_type=jnp.float32)
    total = total + jnp.dot(weight_up[1], weight_down[1], preferred_element_type=jnp.float32)
    return jnp.eye(weight_up.shape[1], dtype=jnp.float32) + GAMMA * total


def shards(token_ids, embedding, w_up, w_down, cotangent):
    depth = lax.axis_size("depth")
    position = lax.axis_index("depth")
    first = position == 0
    final_block = position == depth - 1
    layers = w_up.shape[0]
    vocab_rows = embedding.shape[0]
    local_ids = token_ids - position * vocab_rows
    inside = (local_ids >= 0) & (local_ids < vocab_rows)
    picked = jnp.take(embedding, jnp.clip(local_ids, 0, vocab_rows - 1), axis=0)
    picked = jnp.where(inside[:, None], picked, jnp.zeros_like(picked)).astype(jnp.float32)
    start = lax.psum(picked.astype(jnp.bfloat16), "depth").astype(jnp.float32)
    matrix = coarse_matrix(w_up, w_down)
    transposed = matrix.T
    zeros = jnp.zeros_like(start)
    coarse = start
    arrived_projection = zeros
    for sweep in range(RELAX):
        run_state = coarse
        for run_layer in range(layers):
            run_state, unused = layer_forward(run_state, w_up[run_layer], w_down[run_layer])
        projection = jnp.dot(coarse, matrix, precision=lax.Precision.HIGHEST)
        arrived, arrived_projection = shifted((run_state, projection), "depth", 1)
        coarse = jnp.where(first, start, arrived)
    tau = coarse - arrived_projection

    def forward_turn(turn, incoming):
        carried = jnp.dot(incoming + tau, matrix, precision=lax.Precision.HIGHEST)
        return shifted(carried.astype(jnp.bfloat16), "depth", 1).astype(carried.dtype)

    incoming = lax.fori_loop(0, depth - 1, forward_turn, zeros)
    corrected = incoming + tau
    states = []
    saves = []
    state = corrected
    for layer in range(layers):
        states.append(state)
        state, saved = layer_forward(state, w_up[layer], w_down[layer])
        saves.append(saved)

    def run_adjoint(adjoint):
        for layer in reversed(range(layers)):
            adjoint, low, delta = layer_adjoint(
                states[layer], saves[layer], adjoint, w_up[layer], w_down[layer]
            )
        return adjoint

    final = cotangent.astype(jnp.float32)
    adjoint_state = final
    back_projection = zeros
    for sweep in range(RELAX):
        begun = run_adjoint(adjoint_state)
        projection = jnp.dot(adjoint_state, transposed, precision=lax.Precision.HIGHEST)
        arrived, back_projection = (
            shifted(begun.astype(jnp.bfloat16), "depth", -1).astype(begun.dtype),
            shifted(projection.astype(jnp.bfloat16), "depth", -1).astype(projection.dtype),
        )
        adjoint_state = jnp.where(final_block, final, arrived)
    back_tau = adjoint_state - back_projection

    def backward_turn(turn, incoming):
        carried = jnp.dot(incoming + back_tau, transposed, precision=lax.Precision.HIGHEST)
        return shifted(carried.astype(jnp.bfloat16), "depth", -1).astype(carried.dtype)

    back_incoming = lax.fori_loop(0, depth - 1, backward_turn, zeros)
    adjoint = back_incoming + back_tau
    lows = [None] * layers
    deltas = [None] * layers
    for layer in reversed(range(layers)):
        adjoint, low, delta = layer_adjoint(
            states[layer], saves[layer], adjoint, w_up[layer], w_down[layer]
        )
        lows[layer] = low
        deltas[layer] = delta
    local_up = jnp.stack(
        [
            lax.dot_general(
                saves[layer][1],
                deltas[layer],
                (((0,), (0,)), ((), ())),
                preferred_element_type=jnp.float32,
            )
            for layer in range(layers)
        ],
        0,
    )
    local_down = jnp.stack(
        [
            lax.dot_general(
                saves[layer][3],
                lows[layer],
                (((0,), (0,)), ((), ())),
                preferred_element_type=jnp.float32,
            )
            for layer in range(layers)
        ],
        0,
    )
    grad_up, grad_down = (
        lax.psum_scatter(
            local_up.astype(jnp.bfloat16), "dp", scatter_dimension=1, tiled=True
        ).astype(jnp.float32),
        lax.psum_scatter(
            local_down.astype(jnp.bfloat16), "dp", scatter_dimension=1, tiled=True
        ).astype(jnp.float32),
    )
    return (grad_up, grad_down)


def solution(mesh):
    in_specs = (
        P("dp"),
        P("depth", None),
        P("depth", None, None),
        P("depth", None, None),
        P("dp", None),
    )
    out_specs = (P("depth", "dp", None), P("depth", "dp", None))
    return jax.shard_map(shards, mesh=mesh, in_specs=in_specs, out_specs=out_specs, check_vma=False)
```

profile of v0, /device:TPU:8, one launch (start us, length us, event | category | flops | bytes accessed | tf_op | source)
XLA Modules:
  0.0 967.2 jit_solution(8096644310616206722)
XLA Ops:
  10.2 121.4 %all-reduce.2.cloned.1.call-done = bf16[128,512]{1,0:T(8,128)(2,1)} async-done(((bf16[128,512]{1,0:T(8,128)(2,1)}), bf16[128,512]{1,0:T(8,128)(2,1)}) %all-reduce.2.cloned.1.call-update) | async-done | bytes 131088 | tf_op jit(solution)/shard_map/psum | solution.py:61
  140.8 4.5 fusion.30
  184.5 119.6 %while.22 = (s32[]{:T(128)}, f32[128,512]{1,0:T(8,128)S(1)}, f32[128,512]{1,0:T(8,128)S(1)}, f32[512,512]{1,0:T(8,128)S(1)}, s32[]{:T(128)}, /*index=5*/s32[]{:T(128)}) while((s32[]{:T(128)}, f32[128,512]{1,0:T(8,128)S(1)}, f32[128,512]{1,0:T(8,128)S(1)}, f32[512,512]{1,0:T(8,128)S(1)}, s32[]{:T(128)}, /*index=5*/s32[]{:T(128)}) %tuple.59), condition=%wide.region_8.9_spmd.clone, body=%wide.region_7.8_spmd.clone.sunk | while | flops 402915328 | bytes 2621559 | solution.py:80
  241.8 6.2 collective-permute-start
  249.7 7.4 collective-permute-start
  258.9 7.4 collective-permute-start
  268.1 7.4 collective-permute-start
  277.3 7.4 collective-permute-start
  286.4 7.4 collective-permute-start
  295.6 7.4 collective-permute-start
  321.9 6.5 collective-permute-done.6
  339.6 7.2 collective-permute-done.7
  351.1 4.9 multiply_reduce_fusion.1
  369.2 139.0 %while.23 = (s32[]{:T(128)}, f32[128,512]{1,0:T(8,128)S(1)}, f32[128,512]{1,0:T(8,128)S(1)}, f32[512,512]{1,0:T(8,128)S(1)}, s32[]{:T(128)}, /*index=5*/s32[]{:T(128)}) while((s32[]{:T(128)}, f32[128,512]{1,0:T(8,128)S(1)}, f32[128,512]{1,0:T(8,128)S(1)}, f32[512,512]{1,0:T(8,128)S(1)}, s32[]{:T(128)}, ...), condition=%wide.region_18.19_spmd.clone, body=%wide.region_17.18_spmd.clone.sunk | while | flops 402915328 | bytes 2621559 | solution.py:114
  371.9 7.2 collective-permute-done.1
  381.8 6.3 collective-permute-done.1
  390.8 7.2 collective-permute-done.1
  400.7 6.5 collective-permute-done.1
  409.9 6.5 collective-permute-done.1
  419.0 6.5 collective-permute-done.1
  428.2 6.5 collective-permute-done.1
  437.4 6.5 collective-permute-done.1
  446.6 6.5 collective-permute-done.1
  455.8 6.5 collective-permute-done.1
  464.9 6.5 collective-permute-done.1
  474.1 6.5 collective-permute-done.1
  483.3 6.5 collective-permute-done.1
  492.5 6.5 collective-permute-done.1
  501.7 6.5 collective-permute-done.1
  519.6 4.9 fusion.6
  528.4 219.8 %reduce-scatter.5.cloned.1.call-done = bf16[2,128,512]{2,1,0:T(8,128)(2,1)} async-done(((bf16[2,2048,512]{2,1,0:T(8,128)(2,1)}), bf16[2,128,512]{2,1,0:T(8,128)(2,1)}) %reduce-scatter.5.cloned.1.call-update) | async-done | bytes 262160 | tf_op jit(solution)/shard_map/reduce_scatter | solution.py:152
  750.0 208.9 %reduce-scatter.3.cloned.1.call-done = bf16[2,32,2048]{2,1,0:T(8,128)(2,1)} async-done(((bf16[2,512,2048]{2,1,0:T(8,128)(2,1)}), bf16[2,32,2048]{2,1,0:T(8,128)(2,1)}) %reduce-scatter.3.cloned.1.call-update) | async-done | bytes 262160 | tf_op jit(solution)/shard_map/reduce_scatter | solution.py:149
  (210 shorter events, 224.9 us)
Async XLA Ops:
  7.2 124.4 %all-reduce.2.cloned.1.call-start = ((), (), s32[]{:S(2)}) async-start(), calls=%async_computation.2 | async-start | bytes 262144 | tf_op jit(solution)/shard_map/psum | solution.py:61
  10.1 738.1 %reduce-scatter.5.cloned.1.call-start = ((), (), s32[]{:S(2)}) async-start(), calls=%async_computation.4 | async-start | bytes 4456448 | tf_op jit(solution)/shard_map/reduce_scatter | solution.py:152
  138.8 9.2 collective-permute-start.2
  154.9 7.9 collective-permute-start.3
  171.2 8.0 collective-permute-start.4
  175.6 7.9 collective-permute-start.5
  249.7 8.4 collective-permute-start
  258.9 8.4 collective-permute-start
  268.1 8.4 collective-permute-start
  277.3 8.4 collective-permute-start
  286.4 8.4 collective-permute-start
  295.6 8.4 collective-permute-start
  319.9 8.4 collective-permute-start.6
  337.7 9.1 collective-permute-start.7
  357.8 8.5 collective-permute-start.8
  360.9 8.3 collective-permute-start.9
  369.9 9.1 collective-permute-start.1
  379.8 8.3 collective-permute-start.1
  388.9 9.1 collective-permute-start.1
  398.8 8.4 collective-permute-start.1
  408.0 8.4 collective-permute-start.1
  417.1 8.4 collective-permute-start.1
  426.3 8.4 collective-permute-start.1
  435.5 8.4 collective-permute-start.1
  444.7 8.4 collective-permute-start.1
  453.9 8.4 collective-permute-start.1
  463.0 8.4 collective-permute-start.1
  472.2 8.4 collective-permute-start.1
  481.4 8.4 collective-permute-start.1
  490.6 8.4 collective-permute-start.1
  499.7 8.4 collective-permute-start.1
  517.4 441.5 %reduce-scatter.3.cloned.1.call-start = ((), (), s32[]{:S(2)}) async-start(), calls=%async_computation.3 | async-start | bytes 4456448 | tf_op jit(solution)/shard_map/reduce_scatter | solution.py:149
  (24 other events, 195.4 us)
Sparse Core Ops, SparseCore 0:
  11.2 120.3 all-reduce.1
  517.5 230.6 reduce-scatter.4
  752.2 206.5 reduce-scatter.2
where the time goes:
time: 969 us; the launch traced here: 967 us
  waiting for transfers between devices  716 us (74%)
  starting transfers between devices  113 us (12%)
  matrix products  96.1 us (10%)
  other arithmetic  19.6 us (2%)
  between operations  14.2 us (1%)
    reduce_scatter x1, waiting for transfers between devices, shards(): lax.psum_scatter(local_down.astype(jnp.bfloat16), 'dp', scatter_dimension...  220 us
    reduce_scatter x1, waiting for transfers between devices, shards(): lax.psum_scatter(local_up.astype(jnp.bfloat16), 'dp', scatter_dimension=1...  209 us
    ppermute x38, waiting for transfers between devices, shifted(): return lax.ppermute(block, axis, route)  166 us
    psum x1, waiting for transfers between devices, shards(): start = lax.psum(picked.astype(jnp.bfloat16), 'depth').astype(jnp.float32)  121 us
    ppermute x38, starting transfers between devices, shifted(): return lax.ppermute(block, axis, route)  113 us
    dot_general x7, matrix products, layer_adjoint(): lax.dot_general(delta, weight_up, (((1,), (1,)), ((), ())), preferred_ele...  26.2 us
    dot_general x7, matrix products, layer_forward(): jnp.dot(hidden, weight_down, preferred_element_type=jnp.float32)  21.1 us
  transfers between devices with their start and end apart: 41, of which 41 were waited for; matrix products, arithmetic and copies ran while one was open for 3% of the time, Pallas kernels for 0%

commit v1 on v0

v1 whole, which is shorter than its diff:
```python
import functools

import jax
import jax.numpy as jnp
from jax import lax
from jax.experimental import pallas as pl
from jax.experimental.pallas import tpu as pltpu
from jax.sharding import PartitionSpec as P

RELAX = 3
EPSILON = 1e-06
GAMMA = 0.05
F32, BF16 = jnp.float32, jnp.bfloat16
MESH = pl.DeviceIdType.MESH


def nn(a, b):
    return jnp.dot(a, b, preferred_element_type=F32)


def nt(a, b):
    return lax.dot_general(a, b, (((1,), (1,)), ((), ())), preferred_element_type=F32)


def sigmoid(p):
    return 0.5 * jnp.tanh(0.5 * p) + 0.5


def kernel(
    nd, nz,
    tok, emb, wu_hbm, wd_hbm, cot,
    gu_out, gd_out,
    wu, wd,
    epick, erecv, estart,
    own_d, pair_d, all_n,
    cbuf, fsend, abuf, asend,
    tsend, tpair, usend, ubuf, ysend, ybuf,
    bsend, bpair, wsend, wbuf, zsend, zbuf,
    corr, unit, scales, slope,
    rbuf, wus, wds, norm_t, hid_t, slope_s,
    gu, gd, gus, gds, gurecv, gdrecv,
    load_sem, e_s, e_r, e2_s, e2_r, d_s, d_r, n_s, n_r,
    f_s, f_r, a_s, a_r, t_s, t_r, u_s, u_r, y_s, y_r,
    b_s, b_r, w_s, w_r, z_s, z_r, ring_s, ring_r, g_s, g_r, h_s, h_r,
):
    T, D = cot.shape
    L, _, FF = wu.shape
    ndp, nchip = 2 * nz, nd // 2
    k, p = lax.axis_index("depth"), lax.axis_index("dp")
    core, chip = k % 2, k // 2
    x, z = p // nz, p % nz
    F = FF // ndp
    vocab = emb.shape[0]
    wide = min(512, FF)

    def remote(src, dst, ssem, rsem, depth=k, dp=p):
        return pltpu.make_async_remote_copy(
            src_ref=src, dst_ref=dst, send_sem=ssem, recv_sem=rsem,
            device_id={"depth": depth, "dp": dp}, device_id_type=MESH,
        )

    load_up = pltpu.make_async_copy(wu_hbm, wu, load_sem.at[0])
    load_down = pltpu.make_async_copy(wd_hbm, wd, load_sem.at[1])
    load_up.start()
    load_down.start()

    barrier = pltpu.get_barrier_semaphore()

    def greet_depth(i, c):
        pl.semaphore_signal(barrier, inc=1, device_id={"depth": (k + i) % nd, "dp": p}, device_id_type=MESH)
        return c

    def greet_dp(i, c):
        pl.semaphore_signal(barrier, inc=1, device_id={"depth": k, "dp": (p + i) % ndp}, device_id_type=MESH)
        return c

    lax.fori_loop(1, nd, greet_depth, 0)
    lax.fori_loop(1, ndp, greet_dp, 0)

    R, H = T // nchip, D // 2
    local = tok[...] - k * vocab
    onehot = (local == lax.broadcasted_iota(jnp.int32, (T, vocab), 1)).astype(BF16)
    picked = nn(onehot, emb[...]).astype(BF16)
    for c in range(nd):
        epick[c] = picked[(c // 2) * R:(c // 2 + 1) * R, (c % 2) * H:(c % 2 + 1) * H]
    pl.semaphore_wait(barrier, nd + ndp - 2)

    def pick_copy(i):
        t = (k + i) % nd
        return remote(epick.at[t], erecv.at[k], e_s.at[i], e_r.at[k], depth=t)

    def pick_arrival(i):
        t = (k + i) % nd
        return remote(epick.at[t], erecv.at[t], e_s.at[i], e_r.at[t], depth=t)

    def start_copy(i):
        t = (k + i) % nd
        return remote(estart.at[k], estart.at[k], e2_s.at[i], e2_r.at[k], depth=t)

    def start_arrival(i):
        t = (k + i) % nd
        return remote(estart.at[t], estart.at[t], e2_s.at[i], e2_r.at[t], depth=t)

    def each(low, high, f):
        def body(i, c):
            f(i)
            return c
        lax.fori_loop(low, high, body, 0)

    each(1, nd, lambda i: pick_copy(i).start())
    erecv[k] = epick[k]

    load_up.wait()
    load_down.wait()

    def coarse_rows(i):
        rows = pl.ds(pl.multiple_of(i * 128, 128), 128)
        total = nn(wu[0, rows, :], wd[0])
        total = total + nn(wu[1, rows, :], wd[1])
        own_d[rows, :] = (GAMMA * total).astype(BF16)

    each(0, D // 128, coarse_rows)
    d_copy = remote(own_d, pair_d, d_s, d_r, depth=k + 1 - 2 * core)
    d_copy.start()

    each(1, nd, lambda i: pick_arrival(i).wait_recv())
    total = erecv[0].astype(F32)
    for c in range(1, nd):
        total = total + erecv[c].astype(F32)
    estart[k] = total.astype(BF16)
    each(1, nd, lambda i: start_copy(i).start())

    d_copy.wait_recv()

    def n_copy(i):
        t = (chip + i) % nchip
        return remote(all_n.at[chip], all_n.at[chip], n_s.at[i], n_r.at[chip], depth=2 * t)

    def n_arrival(i):
        t = (chip + i) % nchip
        return remote(all_n.at[t], all_n.at[t], n_s.at[i], n_r.at[t], depth=2 * t)

    @pl.when(core == 0)
    def _():
        product = nn(own_d[...], pair_d[...])
        all_n[chip] = (product + own_d[...].astype(F32) + pair_d[...].astype(F32)).astype(BF16)
        each(1, nchip, lambda i: n_copy(i).start())

    for half in range(2):
        at = pl.multiple_of(half * (FF // 2) + z * F, 128)
        for layer in range(L):
            wus[layer, :, half * F:(half + 1) * F] = wu[layer, :, pl.ds(at, F)]
            wds[layer, half * F:(half + 1) * F, :] = wd[layer, pl.ds(at, F), :]

    each(1, nd, lambda i: start_arrival(i).wait_recv())
    for c in range(nd):
        cbuf[0, (c // 2) * R:(c // 2 + 1) * R, (c % 2) * H:(c % 2 + 1) * H] = estart[c].astype(F32)

    def forward(v, layer, save):
        scale = lax.rsqrt(jnp.mean(v * v, axis=-1, keepdims=True) + EPSILON)
        n = v * scale
        normed = n.astype(BF16)
        if save:
            unit[layer] = n
            scales[layer] = scale
            rbuf[layer, z] = normed
        total = None
        for at in range(0, FF, wide):
            pre = nn(normed, wu[layer, :, at:at + wide])
            s = sigmoid(pre)
            if save:
                slope[layer, :, at:at + wide] = s * (1.0 + pre * (1.0 - s))
            part = nn((pre * s).astype(BF16), wd[layer, at:at + wide, :])
            total = part if total is None else total + part
        return v + total

    def adjoint(g, layer):
        low = g.astype(BF16)
        q = None
        for at in range(0, FF, wide):
            toward = nt(low, wd[layer, at:at + wide, :])
            delta = (toward * slope[layer, :, at:at + wide]).astype(BF16)
            part = nt(delta, wu[layer, :, at:at + wide])
            q = part if q is None else q + part
        n = unit[layer]
        inner = jnp.mean(q * n, axis=-1, keepdims=True)
        return g + scales[layer] * (q - n * inner)

    def f_copy(s):
        return remote(fsend.at[s], cbuf.at[s + 1], f_s.at[s], f_r.at[s], depth=(k + 1) % nd)

    def forward_sweep(s):
        v = cbuf[s]
        for layer in range(L):
            v = forward(v, layer, False)
        fsend[s] = v

        @pl.when(k < nd - 1)
        def _():
            f_copy(s).start()

        @pl.when(k > 0)
        def _():
            f_copy(s).wait_recv()

        @pl.when(k == 0)
        def _():
            cbuf[s + 1] = cbuf[0]

    each(0, RELAX, forward_sweep)

    def times(v, d):
        return v + nn(v.astype(BF16), d)

    def times_t(v, d):
        return v + nt(v.astype(BF16), d)

    t_copy = remote(tsend, tpair, t_s, t_r, depth=k + 1 - 2 * core)

    def u_copy(c):
        return remote(usend.at[pl.ds(c * R, R)], ubuf.at[chip], u_s.at[c], u_r.at[chip], depth=2 * c)

    def u_arrival(c):
        return remote(usend.at[pl.ds(c * R, R)], ubuf.at[c], u_s.at[c], u_r.at[c], depth=2 * c)

    def y_copy(src, dst, ss, rs, c, to):
        return remote(src.at[c], dst.at[pl.ds(pl.multiple_of(chip * R, R), R)], ss.at[c, to], rs.at[chip], depth=2 * c + to)

    def y_arrival(src, dst, ss, rs, c):
        return remote(src.at[c], dst.at[pl.ds(c * R, R)], ss.at[c, 0], rs.at[c], depth=2 * c)

    def give(src, dst, ss, rs, c):
        y_copy(src, dst, ss, rs, c, 1).start()

        @pl.when(chip != c)
        def _():
            y_copy(src, dst, ss, rs, c, 0).start()

        @pl.when(chip == c)
        def _():
            dst[pl.ds(pl.multiple_of(chip * R, R), R), :] = src[c]

    def take(src, dst, ss, rs):
        for c in range(nchip):
            @pl.when((core == 1) | (chip != c))
            def _(c=c):
                y_arrival(src, dst, ss, rs, c).wait_recv()

    change = cbuf[RELAX] - cbuf[RELAX - 1]

    @pl.when(core == 0)
    def _():
        tsend[...] = times(change, own_d[...]).astype(BF16)
        t_copy.start()
        each(1, nchip, lambda i: n_arrival(i).wait_recv())
        for c in range(nchip):
            u_arrival(c).wait_recv()
        y = jnp.zeros((R, D), F32)
        for c in range(nchip):
            ysend[c] = y.astype(BF16)
            give(ysend, ybuf, y_s, y_r, c)
            if c < nchip - 1:
                y = times(y, all_n[c]) + ubuf[c].astype(F32)
        take(ysend, ybuf, y_s, y_r)
        corr[...] = cbuf[RELAX] + ybuf[...].astype(F32)

    @pl.when(core == 1)
    def _():
        t_copy.wait_recv()
        usend[...] = times(change + tpair[...].astype(F32), own_d[...]).astype(BF16)
        for c in range(nchip):
            u_copy(c).start()
        take(ysend, ybuf, y_s, y_r)
        corr[...] = (
            cbuf[RELAX] + tpair[...].astype(F32) + times(ybuf[...].astype(F32), pair_d[...])
        )

    steps = ((nz // 2, nz - 1 - nz // 2), (nz - 1 - nz // 2, nz // 2))
    most = nz // 2

    def ring_copy(r, way, s):
        slot = (z - s + nz) % nz if way == 0 else (z + s) % nz
        to = (z + 1) % nz if way == 0 else (z + nz - 1) % nz
        return remote(rbuf.at[r, slot], rbuf.at[r, slot], ring_s.at[r, way, s], ring_r.at[r, way, s], dp=x * nz + to)

    def ring_slot(way, s):
        return (z - s - 1 + nz) % nz if way == 0 else (z + s + 1) % nz

    def ring_arrival(r, way, s):
        slot = ring_slot(way, s)
        to = (z + 1) % nz if way == 0 else (z + nz - 1) % nz
        return remote(rbuf.at[r, slot], rbuf.at[r, slot], ring_s.at[r, way, s], ring_r.at[r, way, s], dp=x * nz + to)

    def ring_begin(r):
        for way in range(2):
            if steps[r % 2][way] > 0:
                ring_copy(r, way, 0).start()

    def ring_step(r, s):
        for way in range(2):
            if s < steps[r % 2][way]:
                ring_arrival(r, way, s).wait_recv()
                if s + 1 < steps[r % 2][way]:
                    ring_copy(r, way, s + 1).start()

    def ring_end(r):
        for way in range(2):
            for s in range(steps[r % 2][way]):
                ring_copy(r, way, s).wait_send()

    v = corr[...]
    for layer in range(L):
        v = forward(v, layer, True)
        ring_begin(layer)

    def a_copy(s):
        return remote(asend.at[s], abuf.at[s + 1], a_s.at[s], a_r.at[s], depth=(k + nd - 1) % nd)

    abuf[0] = cot[...]

    for s in range(RELAX):
        g = abuf[s].astype(F32)
        for layer in reversed(range(L)):
            g = adjoint(g, layer)
        asend[s] = g.astype(BF16)

        @pl.when(k > 0)
        def _():
            a_copy(s).start()

        if s < most:
            ring_step(0, s)
            ring_step(1, s)

        @pl.when(k < nd - 1)
        def _():
            a_copy(s).wait_recv()

        @pl.when(k == nd - 1)
        def _():
            abuf[s + 1] = abuf[0]

    b_copy = remote(bsend, bpair, b_s, b_r, depth=k + 1 - 2 * core)

    def w_copy(c):
        return remote(wsend.at[pl.ds(c * R, R)], wbuf.at[chip], w_s.at[c], w_r.at[chip], depth=2 * c)

    def w_arrival(c):
        return remote(wsend.at[pl.ds(c * R, R)], wbuf.at[c], w_s.at[c], w_r.at[c], depth=2 * c)

    change = abuf[RELAX].astype(F32) - abuf[RELAX - 1].astype(F32)

    @pl.when(core == 1)
    def _():
        bsend[...] = times_t(change, own_d[...]).astype(BF16)
        b_copy.start()

    for s in range(RELAX, most):
        ring_step(0, s)
        ring_step(1, s)

    def prepare(j):
        for layer in range(L):
            normed = rbuf[layer, j]
            norm_t[layer, j] = normed.T
            pre = nn(normed, wus[layer])
            s = sigmoid(pre)
            hid_t[layer, j] = (pre * s).astype(BF16).T
            slope_s[layer, j] = s * (1.0 + pre * (1.0 - s))

    @pl.when(core == 0)
    def _():
        b_copy.wait_recv()
        wsend[...] = times_t(change + bpair[...].astype(F32), own_d[...]).astype(BF16)
        for c in range(nchip):
            @pl.when(chip != c)
            def _(c=c):
                w_copy(c).start()

            @pl.when(chip == c)
            def _(c=c):
                wbuf[c] = wsend[c * R:(c + 1) * R, :]

        for c in range(nchip):
            @pl.when(chip != c)
            def _(c=c):
                w_arrival(c).wait_recv()
        y = jnp.zeros((R, D), F32)
        for c in reversed(range(nchip)):
            zsend[c] = y.astype(BF16)
            give(zsend, zbuf, z_s, z_r, c)
            if c > 0:
                y = times_t(y, all_n[c]) + wbuf[c].astype(F32)

    each(0, nz, prepare)

    @pl.when(core == 0)
    def _():
        take(zsend, zbuf, z_s, z_r)
        corr[...] = (
            abuf[RELAX].astype(F32) + bpair[...].astype(F32) + times_t(zbuf[...].astype(F32), pair_d[...])
        )

    @pl.when(core == 1)
    def _():
        take(zsend, zbuf, z_s, z_r)
        corr[...] = abuf[RELAX].astype(F32) + zbuf[...].astype(F32)

    g = corr[...]
    rbuf[L + 1, z] = g.astype(BF16)
    ring_begin(L + 1)
    g = adjoint(g, 1)
    rbuf[L, z] = g.astype(BF16)
    ring_begin(L)

    gu[...] = jnp.zeros_like(gu)
    gd[...] = jnp.zeros_like(gd)

    def contract(layer, j):
        low = rbuf[L + layer, j]
        delta = (nt(low, wds[layer]) * slope_s[layer, j]).astype(BF16)
        gu[layer] += nn(norm_t[layer, j], delta)
        gd[layer] += nn(hid_t[layer, j], low)

    contract(1, z)
    contract(0, z)
    for s in range(most):
        for layer in (1, 0):
            ring_step(L + layer, s)
        for layer in (1, 0):
            for way in range(2):
                if s < steps[layer][way]:
                    contract(layer, ring_slot(way, s))

    rows = D // ndp

    def g_copy(layer, i):
        t = (p + i) % ndp
        return remote(
            gus.at[layer, pl.ds(pl.multiple_of(t * rows, rows), rows)], gurecv.at[layer, p],
            g_s.at[layer, i], g_r.at[layer, p], dp=t,
        )

    def g_arrival(layer, i):
        t = (p + i) % ndp
        return remote(
            gus.at[layer, pl.ds(pl.multiple_of(t * rows, rows), rows)], gurecv.at[layer, t],
            g_s.at[layer, i], g_r.at[layer, t], dp=t,
        )

    def h_copy(layer):
        return remote(
            gds.at[layer, pl.ds(pl.multiple_of((1 - x) * F, F), F)], gdrecv.at[layer],
            h_s.at[layer], h_r.at[layer], dp=(1 - x) * nz + z,
        )

    for layer in (1, 0):
        gus[layer] = gu[layer].astype(BF16)
        each(1, ndp, lambda i: g_copy(layer, i).start())
        gds[layer] = gd[layer].astype(BF16)
        h_copy(layer).start()
        gurecv[layer, p] = gus[layer, pl.ds(pl.multiple_of(p * rows, rows), rows), :]

    for layer in (1, 0):
        h_copy(layer).wait_recv()
        gd_out[layer] = gd[layer, pl.ds(pl.multiple_of(x * F, F), F), :] + gdrecv[layer].astype(F32)
        each(1, ndp, lambda i: g_arrival(layer, i).wait_recv())
        for j in range(nz):
            both = gurecv[layer, j].astype(F32) + gurecv[layer, nz + j].astype(F32)
            gu_out[layer, :, j * F:(j + 1) * F] = both[:, :F]
            gu_out[layer, :, FF // 2 + j * F:FF // 2 + (j + 1) * F] = both[:, F:]

    each(1, nd, lambda i: pick_copy(i).wait_send())
    each(1, nd, lambda i: start_copy(i).wait_send())
    d_copy.wait_send()

    @pl.when(k < nd - 1)
    def _():
        each(0, RELAX, lambda s: f_copy(s).wait_send())

    @pl.when(k > 0)
    def _():
        each(0, RELAX, lambda s: a_copy(s).wait_send())

    @pl.when(core == 0)
    def _():
        each(1, nchip, lambda i: n_copy(i).wait_send())
        t_copy.wait_send()
        for src, dst, ss, rs in ((ysend, ybuf, y_s, y_r), (zsend, zbuf, z_s, z_r)):
            for c in range(nchip):
                y_copy(src, dst, ss, rs, c, 1).wait_send()

                @pl.when(chip != c)
                def _():
                    y_copy(src, dst, ss, rs, c, 0).wait_send()

        for c in range(nchip):
            @pl.when(chip != c)
            def _():
                w_copy(c).wait_send()

    @pl.when(core == 1)
    def _():
        b_copy.wait_send()
        for c in range(nchip):
            u_copy(c).wait_send()

    for r in range(2 * L):
        ring_end(r)
    for layer in range(L):
        each(1, ndp, lambda i: g_copy(layer, i).wait_send())
        h_copy(layer).wait_send()


def shards(nd, ndp, token_ids, embedding, w_up, w_down, cotangent):
    T, D = cotangent.shape
    L, _, FF = w_up.shape
    nz, nchip = ndp // 2, nd // 2
    R, F = T // nchip, FF // ndp
    most = max(nz // 2, 1)
    V = pltpu.VMEM
    sem = pltpu.SemaphoreType.DMA
    scratch = [
        V((L, D, FF), BF16), V((L, FF, D), BF16),
        V((nd, R, D // 2), BF16), V((nd, R, D // 2), BF16), V((nd, R, D // 2), BF16),
        V((D, D), BF16), V((D, D), BF16), V((nchip, D, D), BF16),
        V((RELAX + 1, T, D), F32), V((RELAX, T, D), F32), V((RELAX + 1, T, D), BF16), V((RELAX, T, D), BF16),
        V((T, D), BF16), V((T, D), BF16), V((T, D), BF16), V((nchip, R, D), BF16), V((nchip, R, D), BF16), V((T, D), BF16),
        V((T, D), BF16), V((T, D), BF16), V((T, D), BF16), V((nchip, R, D), BF16), V((nchip, R, D), BF16), V((T, D), BF16),
        V((T, D), F32), V((L, T, D), F32), V((L, T, 1), F32), V((L, T, FF), F32),
        V((2 * L, nz, T, D), BF16), V((L, D, 2 * F), BF16), V((L, 2 * F, D), BF16),
        V((L, nz, D, T), BF16), V((L, nz, 2 * F, T), BF16), V((L, nz, T, 2 * F), F32),
        V((L, D, 2 * F), F32), V((L, 2 * F, D), F32), V((L, D, 2 * F), BF16), V((L, 2 * F, D), BF16),
        V((L, ndp, D // ndp, 2 * F), BF16), V((L, F, D), BF16),
        sem((2,)), sem((nd,)), sem((nd,)), sem((nd,)), sem((nd,)), sem, sem, sem((nchip,)), sem((nchip,)),
        sem((RELAX,)), sem((RELAX,)), sem((RELAX,)), sem((RELAX,)),
        sem, sem, sem((nchip,)), sem((nchip,)), sem((nchip, 2)), sem((nchip,)),
        sem, sem, sem((nchip,)), sem((nchip,)), sem((nchip, 2)), sem((nchip,)),
        sem((2 * L, 2, most)), sem((2 * L, 2, most)), sem((L, ndp)), sem((L, ndp)), sem((L,)), sem((L,)),
    ]
    vmem = pl.BlockSpec(memory_space=pltpu.VMEM)
    hbm = pl.BlockSpec(memory_space=pl.ANY)
    return pl.pallas_call(
        functools.partial(kernel, nd, nz),
        out_shape=(
            jax.ShapeDtypeStruct((L, D // ndp, FF), F32),
            jax.ShapeDtypeStruct((L, FF // ndp, D), F32),
        ),
        in_specs=[vmem, vmem, hbm, hbm, vmem],
        out_specs=(vmem, vmem),
        scratch_shapes=scratch,
        compiler_params=pltpu.CompilerParams(
            collective_id=0, has_side_effects=True, vmem_limit_bytes=58 * 1024 * 1024
        ),
    )(token_ids[:, None], embedding, w_up, w_down, cotangent)


def solution(mesh):
    in_specs = (
        P("dp"),
        P("depth", None),
        P("depth", None, None),
        P("depth", None, None),
        P("dp", None),
    )
    out_specs = (P("depth", "dp", None), P("depth", "dp", None))
    body = functools.partial(shards, mesh.shape["depth"], mesh.shape["dp"])
    return jax.shard_map(body, mesh=mesh, in_specs=in_specs, out_specs=out_specs, check_vma=False)
```

time: 969 us -> 150 us (0.15)
  waiting for transfers between devices: 716 us -> 0 us
  Pallas kernels: 0 us -> 144 us
  starting transfers between devices: 113 us -> 0 us
  matrix products: 96.1 us -> 0 us
  other arithmetic: 19.6 us -> 0 us
  between operations: 14.2 us -> 0.64 us
    reduce_scatter x2 -> x0, waiting for transfers between devices: 429 us -> none  [the longest x1 220 us: shards(): lax.psum_scatter(local_down.astype(jnp.bfloat16), 'dp', scatter_dimension...]
    ppermute x38 -> x0, waiting for transfers between devices: 166 us -> none  [shifted(): return lax.ppermute(block, axis, route)]
    pallas_call x0 -> x1, Pallas kernels: none -> 144 us  [shards(): pl.pallas_call(functools.partial(kernel, nd, nz), out_shape=(jax.ShapeDty...]
    psum x1 -> x0, waiting for transfers between devices: 121 us -> none  [shards(): start = lax.psum(picked.astype(jnp.bfloat16), 'depth').astype(jnp.float32)]
    ppermute x38 -> x0, starting transfers between devices: 113 us -> none  [shifted(): return lax.ppermute(block, axis, route)]
    dot_general x55 -> x0, matrix products: 96.1 us -> none  [the longest x7 26.2 us: layer_adjoint(): lax.dot_general(delta, weight_up, (((1,), (1,)), ((), ())), preferred_ele...]
  transfers between devices with their start and end apart: 41 -> 0, of which waited for: 41 -> 0; matrix products, arithmetic and copies ran while one was open for 3% -> 0% of each run, Pallas kernels for 0% -> 0%
where the time goes in v1:
time: 150 us
  Pallas kernels  144 us (96%)
  local copies, waits for them, and re-layouts  5.13 us (3%)
    pallas_call x1, Pallas kernels, shards(): pl.pallas_call(functools.partial(kernel, nd, nz), out_shape=(jax.ShapeDty...  144 us
    unnamed x2, local copies, waits for them, and re-layouts  3.74 us

profile of v1, /device:TPU:8, one launch (start us, length us, event | category | flops | bytes accessed | tf_op | source)
XLA Modules:
  0.0 149.8 jit_solution(4305032992898775956)
XLA Ops:
  0.6 1.4 copy.7.tok
  2.0 144.1 %shard_map.68 = (f32[2,32,2048]{2,1,0:T(8,128)}, f32[2,128,512]{2,1,0:T(8,128)}) custom-call(s32[128,1]{1,0:T(8,128)} %copy.7.tok, bf16[1280,512]{1,0:T(8,128)(2,1)} %emb.1, bf16[2,512,2048]{2,1,0:T(8,128)(2,1)} %wu_hbm.1, bf16[2,2048,512]{2,1,0:T(8,128)(2,1)} %wd_hbm.1, bf16[128,512]{1,0:T(8,128)(2,1)} %cot.1), custom_call_target="tpu_custom_call" | custom-call | tf_op jit(solution)/shard_map/pallas_call | solution.py:543
  146.1 1.9 %copy.10 = f32[2,32,2048]{2,1,0:T(8,128)} copy(f32[2,32,2048]{2,1,0:T(8,128)} %get-tuple-element.4) | data formatting | bytes 1048576
  148.0 1.9 %copy.11 = f32[2,128,512]{2,1,0:T(8,128)} copy(f32[2,128,512]{2,1,0:T(8,128)} %get-tuple-element.5) | data formatting | bytes 1048576

commit v2 on v1

v2 whole, which is shorter than its diff:
```python
import functools

import jax
import jax.numpy as jnp
from jax import lax
from jax.experimental import pallas as pl
from jax.experimental.pallas import tpu as pltpu
from jax.sharding import PartitionSpec as P

RELAX = 3
EPSILON = 1e-06
GAMMA = 0.05
F32, BF16 = jnp.float32, jnp.bfloat16
MESH = pl.DeviceIdType.MESH


def nn(a, b):
    return jnp.dot(a, b, preferred_element_type=F32)


def nt(a, b):
    return lax.dot_general(a, b, (((1,), (1,)), ((), ())), preferred_element_type=F32)


def sigmoid(p):
    return 0.5 * jnp.tanh(0.5 * p) + 0.5


def kernel(
    nd, nz,
    tok, emb_hbm, wu_hbm, wd_hbm, cot,
    gu_out, gd_out,
    wu, wd, emb,
    epick, erecv, estart,
    own_d, pair_d, all_n,
    cbuf, fsend, abuf, asend,
    tsend, tpair, usend, ubuf, ysend, ybuf,
    bsend, bpair, wsend, wbuf, zsend, zbuf,
    corr, unit, scales, slope,
    rbuf, wus, wds, norm_t, hid_t, slope_s,
    gu, gd, gus, gds, gurecv, gdrecv, gx, gsum, csend, crecv,
    load_sem, e_s, e_r, e2_s, e2_r, d_s, d_r, n_s, n_r,
    f_s, f_r, a_s, a_r, t_s, t_r, u_s, u_r, y_s, y_r,
    b_s, b_r, w_s, w_r, z_s, z_r, ring_s, ring_r, g_s, g_r, h_s, h_r, x_s, x_r, c_s, c_r,
):
    T, D = cot.shape
    L, _, FF = wu.shape
    ndp, nchip = 2 * nz, nd // 2
    k, p = lax.axis_index("depth"), lax.axis_index("dp")
    core, chip = k % 2, k // 2
    span = max(nchip // 2, 1)
    half, lane = chip // span, chip % span
    Q = T // span
    x, z = p // nz, p % nz
    F = FF // ndp
    vocab = emb.shape[0]
    wide = min(512, FF)

    def remote(src, dst, ssem, rsem, depth=k, dp=p):
        return pltpu.make_async_remote_copy(
            src_ref=src, dst_ref=dst, send_sem=ssem, recv_sem=rsem,
            device_id={"depth": depth, "dp": dp}, device_id_type=MESH,
        )

    load_up = pltpu.make_async_copy(wu_hbm, wu, load_sem.at[0])
    load_down = pltpu.make_async_copy(wd_hbm, wd, load_sem.at[1])
    load_rows = pltpu.make_async_copy(emb_hbm, emb, load_sem.at[2])
    load_rows.start()
    load_up.start()
    load_down.start()

    barrier = pltpu.get_barrier_semaphore()
    pending = []

    def greet_depth(i, c):
        pl.semaphore_signal(barrier, inc=1, device_id={"depth": (k + i) % nd, "dp": p}, device_id_type=MESH)
        return c

    def greet_dp(i, c):
        pl.semaphore_signal(barrier, inc=1, device_id={"depth": k, "dp": (p + i) % ndp}, device_id_type=MESH)
        return c

    lax.fori_loop(1, nd, greet_depth, 0)
    lax.fori_loop(1, ndp, greet_dp, 0)

    R, H = T // nchip, D // 2
    load_rows.wait()
    local = jnp.broadcast_to(tok[...] - k * vocab, (T, T)).T[:, :1]
    onehot = (local == lax.broadcasted_iota(jnp.int32, (T, vocab), 1)).astype(BF16)
    picked = nn(onehot, emb[...]).astype(BF16)
    for c in range(nd):
        epick[c] = picked[(c // 2) * R:(c // 2 + 1) * R, (c % 2) * H:(c % 2 + 1) * H]
    pl.semaphore_wait(barrier, nd + ndp - 2)

    def pick_copy(i):
        t = (k + i) % nd
        return remote(epick.at[t], erecv.at[k], e_s.at[i], e_r.at[k], depth=t)

    def pick_arrival(i):
        t = (k + i) % nd
        return remote(epick.at[t], erecv.at[t], e_s.at[i], e_r.at[t], depth=t)

    def start_copy(i):
        t = (k + i) % nd
        return remote(estart.at[k], estart.at[k], e2_s.at[i], e2_r.at[k], depth=t)

    def start_arrival(i):
        t = (k + i) % nd
        return remote(estart.at[t], estart.at[t], e2_s.at[i], e2_r.at[t], depth=t)

    def each(low, high, f):
        def body(i, c):
            f(i)
            return c
        lax.fori_loop(low, high, body, 0)

    each(1, nd, lambda i: pick_copy(i).start())
    pending.append(lambda: each(1, nd, lambda i: pick_copy(i).wait_send()))
    erecv[k] = epick[k]

    load_up.wait()
    load_down.wait()

    def coarse_rows(i):
        rows = pl.ds(pl.multiple_of(i * 128, 128), 128)
        total = nn(wu[0, rows, :], wd[0])
        total = total + nn(wu[1, rows, :], wd[1])
        own_d[rows, :] = (GAMMA * total).astype(BF16)

    each(0, D // 128, coarse_rows)
    d_copy = remote(own_d, pair_d, d_s, d_r, depth=k + 1 - 2 * core)
    d_copy.start()
    pending.append(d_copy.wait_send)

    each(1, nd, lambda i: pick_arrival(i).wait_recv())
    total = erecv[0].astype(F32)
    for c in range(1, nd):
        total = total + erecv[c].astype(F32)
    estart[k] = total.astype(BF16)
    each(1, nd, lambda i: start_copy(i).start())
    pending.append(lambda: each(1, nd, lambda i: start_copy(i).wait_send()))

    d_copy.wait_recv()

    def n_copy(i):
        t = (lane + i) % span
        return remote(all_n.at[lane], all_n.at[lane], n_s.at[i], n_r.at[lane], depth=2 * (half * span + t))

    def n_arrival(i):
        t = (lane + i) % span
        return remote(all_n.at[t], all_n.at[t], n_s.at[i], n_r.at[t], depth=2 * (half * span + t))

    @pl.when(core == 0)
    def _():
        product = nn(own_d[...], pair_d[...])
        all_n[lane] = (product + own_d[...].astype(F32) + pair_d[...].astype(F32)).astype(BF16)
        each(1, span, lambda i: n_copy(i).start())

    def on(condition, f):
        pending.append(lambda: pl.when(condition)(f))

    on(core == 0, lambda: each(1, span, lambda i: n_copy(i).wait_send()))

    for piece in range(2):
        at = pl.multiple_of(piece * (FF // 2) + z * F, 128)
        for layer in range(L):
            wus[layer, :, piece * F:(piece + 1) * F] = wu[layer, :, pl.ds(at, F)]
            wds[layer, piece * F:(piece + 1) * F, :] = wd[layer, pl.ds(at, F), :]

    each(1, nd, lambda i: start_arrival(i).wait_recv())
    for c in range(nd):
        cbuf[0, (c // 2) * R:(c // 2 + 1) * R, (c % 2) * H:(c % 2 + 1) * H] = estart[c]

    def forward(v, layer, save):
        scale = lax.rsqrt(jnp.mean(v * v, axis=-1, keepdims=True) + EPSILON)
        n = v * scale
        normed = n.astype(BF16)
        if save:
            unit[layer] = n
            scales[layer] = scale
            rbuf[layer, z] = normed
        total = None
        for at in range(0, FF, wide):
            pre = nn(normed, wu[layer, :, at:at + wide])
            s = sigmoid(pre)
            if save:
                slope[layer, :, at:at + wide] = s * (1.0 + pre * (1.0 - s))
            part = nn((pre * s).astype(BF16), wd[layer, at:at + wide, :])
            total = part if total is None else total + part
        return v + total

    def adjoint(g, layer):
        low = g.astype(BF16)
        q = None
        for at in range(0, FF, wide):
            toward = nt(low, wd[layer, at:at + wide, :])
            delta = (toward * slope[layer, :, at:at + wide]).astype(BF16)
            part = nt(delta, wu[layer, :, at:at + wide])
            q = part if q is None else q + part
        n = unit[layer]
        inner = jnp.mean(q * n, axis=-1, keepdims=True)
        return g + scales[layer] * (q - n * inner)

    def f_copy(s):
        return remote(fsend.at[s], cbuf.at[s + 1], f_s.at[s], f_r.at[s], depth=(k + 1) % nd)

    def forward_sweep(s):
        v = cbuf[s].astype(F32)
        for layer in range(L):
            v = forward(v, layer, False)
        fsend[s] = v.astype(BF16)

        @pl.when(k < nd - 1)
        def _():
            f_copy(s).start()

        @pl.when(k > 0)
        def _():
            f_copy(s).wait_recv()

        @pl.when(k == 0)
        def _():
            cbuf[s + 1] = cbuf[0]

    each(0, RELAX, forward_sweep)
    on(k < nd - 1, lambda: each(0, RELAX, lambda s: f_copy(s).wait_send()))

    def times(v, d):
        return v + nn(v.astype(BF16), d)

    def times_t(v, d):
        return v + nt(v.astype(BF16), d)

    t_copy = remote(tsend, tpair, t_s, t_r, depth=k + 1 - 2 * core)

    def rows_of(c):
        return pl.ds(c * Q, Q)

    def u_copy(c):
        return remote(usend.at[rows_of(c)], ubuf.at[lane], u_s.at[c], u_r.at[lane], depth=2 * (half * span + c))

    def u_arrival(c):
        return remote(usend.at[rows_of(c)], ubuf.at[c], u_s.at[c], u_r.at[c], depth=2 * (half * span + c))

    mine = pl.ds(pl.multiple_of(lane * Q, Q), Q)

    def y_copy(src, dst, ss, rs, c, to):
        return remote(src.at[c], dst.at[mine], ss.at[c, to], rs.at[lane], depth=2 * (half * span + c) + to)

    def y_arrival(src, dst, ss, rs, c):
        return remote(src.at[c], dst.at[rows_of(c)], ss.at[c, 0], rs.at[c], depth=2 * (half * span + c))

    def give(src, dst, ss, rs, c):
        y_copy(src, dst, ss, rs, c, 1).start()

        @pl.when(lane != c)
        def _():
            y_copy(src, dst, ss, rs, c, 0).start()

        @pl.when(lane == c)
        def _():
            dst[mine, :] = src[c]

    def take(src, dst, ss, rs):
        for c in range(span):
            @pl.when((core == 1) | (lane != c))
            def _(c=c):
                y_arrival(src, dst, ss, rs, c).wait_recv()

    across = (k + nchip) % nd
    c_copy = remote(csend.at[0], crecv.at[0], c_s.at[0], c_r.at[0], depth=across)
    c_back = remote(csend.at[1], crecv.at[1], c_s.at[1], c_r.at[1], depth=across)

    change = cbuf[RELAX].astype(F32) - cbuf[RELAX - 1].astype(F32)

    @pl.when(core == 0)
    def _():
        tsend[...] = times(change, own_d[...]).astype(BF16)
        t_copy.start()
        each(1, span, lambda i: n_arrival(i).wait_recv())
        for c in range(span):
            u_arrival(c).wait_recv()

        @pl.when(half == 0)
        def _():
            crecv[0] = jnp.zeros((Q, D), BF16)

        @pl.when(half == 1)
        def _():
            c_copy.wait_recv()

        y = crecv[0].astype(F32)
        for c in range(span):
            ysend[c] = y.astype(BF16)
            give(ysend, ybuf, y_s, y_r, c)
            y = times(y, all_n[c]) + ubuf[c].astype(F32)

        @pl.when(half == 0)
        def _():
            csend[0] = y.astype(BF16)
            c_copy.start()

        take(ysend, ybuf, y_s, y_r)
        corr[...] = cbuf[RELAX].astype(F32) + ybuf[...].astype(F32)

    @pl.when(core == 1)
    def _():
        t_copy.wait_recv()
        usend[...] = times(change + tpair[...].astype(F32), own_d[...]).astype(BF16)
        for c in range(span):
            u_copy(c).start()
        take(ysend, ybuf, y_s, y_r)
        corr[...] = (
            cbuf[RELAX].astype(F32) + tpair[...].astype(F32) + times(ybuf[...].astype(F32), pair_d[...])
        )

    def given(src, dst, ss, rs):
        for c in range(span):
            y_copy(src, dst, ss, rs, c, 1).wait_send()
            pl.when(lane != c)(y_copy(src, dst, ss, rs, c, 0).wait_send)

    def scan_sent():
        t_copy.wait_send()
        given(ysend, ybuf, y_s, y_r)
        pl.when(half == 0)(c_copy.wait_send)

    def u_sent():
        for c in range(span):
            u_copy(c).wait_send()

    on(core == 0, scan_sent)
    on(core == 1, u_sent)

    steps = ((nz // 2, nz - 1 - nz // 2), (nz - 1 - nz // 2, nz // 2))
    most = nz // 2

    def ring_copy(r, way, s):
        slot = (z - s + nz) % nz if way == 0 else (z + s) % nz
        to = (z + 1) % nz if way == 0 else (z + nz - 1) % nz
        return remote(rbuf.at[r, slot], rbuf.at[r, slot], ring_s.at[r, way, s], ring_r.at[r, way, s], dp=x * nz + to)

    def ring_slot(way, s):
        return (z - s - 1 + nz) % nz if way == 0 else (z + s + 1) % nz

    def ring_arrival(r, way, s):
        slot = ring_slot(way, s)
        to = (z + 1) % nz if way == 0 else (z + nz - 1) % nz
        return remote(rbuf.at[r, slot], rbuf.at[r, slot], ring_s.at[r, way, s], ring_r.at[r, way, s], dp=x * nz + to)

    def ring_begin(r):
        pending.append(lambda: ring_end(r))
        for way in range(2):
            if steps[r % 2][way] > 0:
                ring_copy(r, way, 0).start()

    def ring_step(r, s):
        for way in range(2):
            if s < steps[r % 2][way]:
                ring_arrival(r, way, s).wait_recv()
                if s + 1 < steps[r % 2][way]:
                    ring_copy(r, way, s + 1).start()

    def ring_end(r):
        for way in range(2):
            for s in range(steps[r % 2][way]):
                ring_copy(r, way, s).wait_send()

    def prepare(layer, j):
        normed = rbuf[layer, j]
        norm_t[layer, j] = normed.T
        pre = nn(normed, wus[layer])
        s = sigmoid(pre)
        hid_t[layer, j] = (pre * s).astype(BF16).T
        slope_s[layer, j] = s * (1.0 + pre * (1.0 - s))

    def gather_step(s):
        for layer in range(L):
            ring_step(layer, s)
        for layer in range(L):
            for way in range(2):
                if s < steps[layer][way]:
                    prepare(layer, ring_slot(way, s))

    v = corr[...]
    for layer in range(L):
        v = forward(v, layer, True)
        ring_begin(layer)

    def a_copy(s):
        return remote(asend.at[s], abuf.at[s + 1], a_s.at[s], a_r.at[s], depth=(k + nd - 1) % nd)

    abuf[0] = cot[...]

    for s in range(RELAX):
        g = abuf[s].astype(F32)
        for layer in reversed(range(L)):
            g = adjoint(g, layer)
        asend[s] = g.astype(BF16)

        @pl.when(k > 0)
        def _():
            a_copy(s).start()

        if s == 0:
            prepare(0, z)
            prepare(1, z)
        if s < most:
            gather_step(s)

        @pl.when(k < nd - 1)
        def _():
            a_copy(s).wait_recv()

        @pl.when(k == nd - 1)
        def _():
            abuf[s + 1] = abuf[0]

    on(k > 0, lambda: each(0, RELAX, lambda s: a_copy(s).wait_send()))

    b_copy = remote(bsend, bpair, b_s, b_r, depth=k + 1 - 2 * core)

    def w_copy(c):
        return remote(wsend.at[rows_of(c)], wbuf.at[lane], w_s.at[c], w_r.at[lane], depth=2 * (half * span + c))

    def w_arrival(c):
        return remote(wsend.at[rows_of(c)], wbuf.at[c], w_s.at[c], w_r.at[c], depth=2 * (half * span + c))

    change = abuf[RELAX].astype(F32) - abuf[RELAX - 1].astype(F32)

    @pl.when(core == 1)
    def _():
        bsend[...] = times_t(change, own_d[...]).astype(BF16)
        b_copy.start()

    for s in range(RELAX, most):
        gather_step(s)

    @pl.when(core == 0)
    def _():
        b_copy.wait_recv()
        wsend[...] = times_t(change + bpair[...].astype(F32), own_d[...]).astype(BF16)
        for c in range(span):
            @pl.when(lane != c)
            def _(c=c):
                w_copy(c).start()

            @pl.when(lane == c)
            def _(c=c):
                wbuf[c] = wsend[rows_of(c), :]

        for c in range(span):
            @pl.when(lane != c)
            def _(c=c):
                w_arrival(c).wait_recv()

        @pl.when(half == 1)
        def _():
            crecv[1] = jnp.zeros((Q, D), BF16)

        @pl.when(half == 0)
        def _():
            c_back.wait_recv()

        y = crecv[1].astype(F32)
        for c in reversed(range(span)):
            zsend[c] = y.astype(BF16)
            give(zsend, zbuf, z_s, z_r, c)
            y = times_t(y, all_n[c]) + wbuf[c].astype(F32)

        @pl.when(half == 1)
        def _():
            csend[1] = y.astype(BF16)
            c_back.start()

        take(zsend, zbuf, z_s, z_r)
        corr[...] = (
            abuf[RELAX].astype(F32) + bpair[...].astype(F32) + times_t(zbuf[...].astype(F32), pair_d[...])
        )

    @pl.when(core == 1)
    def _():
        take(zsend, zbuf, z_s, z_r)
        corr[...] = abuf[RELAX].astype(F32) + zbuf[...].astype(F32)

    def w_sent():
        given(zsend, zbuf, z_s, z_r)
        for c in range(span):
            pl.when(lane != c)(w_copy(c).wait_send)
        pl.when(half == 1)(c_back.wait_send)

    on(core == 0, w_sent)
    on(core == 1, b_copy.wait_send)

    g = corr[...]
    rbuf[L + 1, z] = g.astype(BF16)
    ring_begin(L + 1)
    g = adjoint(g, 1)
    rbuf[L, z] = g.astype(BF16)
    ring_begin(L)

    gu[...] = jnp.zeros_like(gu)
    gd[...] = jnp.zeros_like(gd)

    def contract(layer, j):
        low = rbuf[L + layer, j]
        delta = (nt(low, wds[layer]) * slope_s[layer, j]).astype(BF16)
        gu[layer] += nn(norm_t[layer, j], delta)
        gd[layer] += nn(hid_t[layer, j], low)

    rows, part = D // ndp, D // 2
    other = (1 - x) * nz + z

    def x_copy(layer):
        return remote(
            gus.at[layer, pl.ds(pl.multiple_of((1 - x) * part, part), part)], gx.at[layer],
            x_s.at[layer], x_r.at[layer], dp=other,
        )

    def h_copy(layer):
        return remote(
            gds.at[layer, pl.ds(pl.multiple_of((1 - x) * F, F), F)], gdrecv.at[layer],
            h_s.at[layer], h_r.at[layer], dp=other,
        )

    def g_copy(layer, i):
        t = (z + i) % nz
        return remote(
            gsum.at[layer, pl.ds(pl.multiple_of(t * rows, rows), rows)], gurecv.at[layer, z],
            g_s.at[layer, i], g_r.at[layer, z], dp=x * nz + t,
        )

    def g_arrival(layer, i):
        t = (z + i) % nz
        return remote(
            gsum.at[layer, pl.ds(pl.multiple_of(t * rows, rows), rows)], gurecv.at[layer, t],
            g_s.at[layer, i], g_r.at[layer, t], dp=x * nz + t,
        )

    def send_halves(layer):
        gus[layer] = gu[layer].astype(BF16)
        x_copy(layer).start()
        gds[layer] = gd[layer].astype(BF16)
        h_copy(layer).start()
        pending.append(x_copy(layer).wait_send)
        pending.append(h_copy(layer).wait_send)

    contract(1, z)
    contract(0, z)
    for s in range(most):
        for layer in (1, 0):
            ring_step(L + layer, s)
        for layer in (1, 0):
            for way in range(2):
                if s < steps[layer][way]:
                    contract(layer, ring_slot(way, s))
            if s == most - 1:
                send_halves(layer)

    for layer in (1, 0):
        x_copy(layer).wait_recv()
        gsum[layer] = (gu[layer, pl.ds(pl.multiple_of(x * part, part), part), :] + gx[layer].astype(F32)).astype(BF16)
        each(1, nz, lambda i: g_copy(layer, i).start())
        gurecv[layer, z] = gsum[layer, pl.ds(pl.multiple_of(z * rows, rows), rows), :]
        pending.append(lambda layer=layer: each(1, nz, lambda i: g_copy(layer, i).wait_send()))

    for layer in (1, 0):
        h_copy(layer).wait_recv()
        gd_out[layer] = (
            gd[layer, pl.ds(pl.multiple_of(x * F, F), F), :] + gdrecv[layer].astype(F32)
        ).astype(BF16)
    for layer in (1, 0):
        each(1, nz, lambda i: g_arrival(layer, i).wait_recv())
        for j in range(nz):
            gu_out[layer, :, j * F:(j + 1) * F] = gurecv[layer, j, :, :F]
            gu_out[layer, :, FF // 2 + j * F:FF // 2 + (j + 1) * F] = gurecv[layer, j, :, F:]

    for wait in pending:
        wait()


def shards(nd, ndp, token_ids, embedding, w_up, w_down, cotangent):
    T, D = cotangent.shape
    L, _, FF = w_up.shape
    nz, nchip = ndp // 2, nd // 2
    span = max(nchip // 2, 1)
    R, Q, F = T // nchip, T // span, FF // ndp
    most = max(nz // 2, 1)
    V = pltpu.VMEM
    sem = pltpu.SemaphoreType.DMA
    scratch = [
        V((L, D, FF), BF16), V((L, FF, D), BF16), V(embedding.shape, BF16),
        V((nd, R, D // 2), BF16), V((nd, R, D // 2), BF16), V((nd, R, D // 2), BF16),
        V((D, D), BF16), V((D, D), BF16), V((span, D, D), BF16),
        V((RELAX + 1, T, D), BF16), V((RELAX, T, D), BF16), V((RELAX + 1, T, D), BF16), V((RELAX, T, D), BF16),
        V((T, D), BF16), V((T, D), BF16), V((T, D), BF16), V((span, Q, D), BF16), V((span, Q, D), BF16), V((T, D), BF16),
        V((T, D), BF16), V((T, D), BF16), V((T, D), BF16), V((span, Q, D), BF16), V((span, Q, D), BF16), V((T, D), BF16),
        V((T, D), F32), V((L, T, D), F32), V((L, T, 1), F32), V((L, T, FF), F32),
        V((2 * L, nz, T, D), BF16), V((L, D, 2 * F), BF16), V((L, 2 * F, D), BF16),
        V((L, nz, D, T), BF16), V((L, nz, 2 * F, T), BF16), V((L, nz, T, 2 * F), F32),
        V((L, D, 2 * F), F32), V((L, 2 * F, D), F32), V((L, D, 2 * F), BF16), V((L, 2 * F, D), BF16),
        V((L, nz, D // ndp, 2 * F), BF16), V((L, F, D), BF16), V((L, D // 2, 2 * F), BF16), V((L, D // 2, 2 * F), BF16),
        V((2, Q, D), BF16), V((2, Q, D), BF16),
        sem((3,)), sem((nd,)), sem((nd,)), sem((nd,)), sem((nd,)), sem, sem, sem((nchip,)), sem((nchip,)),
        sem((RELAX,)), sem((RELAX,)), sem((RELAX,)), sem((RELAX,)),
        sem, sem, sem((nchip,)), sem((nchip,)), sem((nchip, 2)), sem((nchip,)),
        sem, sem, sem((nchip,)), sem((nchip,)), sem((nchip, 2)), sem((nchip,)),
        sem((2 * L, 2, most)), sem((2 * L, 2, most)), sem((L, nz)), sem((L, nz)), sem((L,)), sem((L,)),
        sem((L,)), sem((L,)), sem((2,)), sem((2,)),
    ]
    vmem = pl.BlockSpec(memory_space=pltpu.VMEM)
    hbm = pl.BlockSpec(memory_space=pl.ANY)
    grad_up, grad_down = pl.pallas_call(
        functools.partial(kernel, nd, nz),
        out_shape=(
            jax.ShapeDtypeStruct((L, D // ndp, FF), BF16),
            jax.ShapeDtypeStruct((L, FF // ndp, D), BF16),
        ),
        in_specs=[vmem, hbm, hbm, hbm, vmem],
        out_specs=(vmem, vmem),
        scratch_shapes=scratch,
        compiler_params=pltpu.CompilerParams(
            collective_id=0, has_side_effects=True, vmem_limit_bytes=58 * 1024 * 1024
        ),
    )(token_ids[None, :], embedding, w_up, w_down, cotangent)
    return grad_up.astype(F32), grad_down.astype(F32)


def solution(mesh):
    in_specs = (
        P("dp"),
        P("depth", None),
        P("depth", None, None),
        P("depth", None, None),
        P("dp", None),
    )
    out_specs = (P("depth", "dp", None), P("depth", "dp", None))
    body = functools.partial(shards, mesh.shape["depth"], mesh.shape["dp"])
    return jax.shard_map(body, mesh=mesh, in_specs=in_specs, out_specs=out_specs, check_vma=False)
```

time: 150 us -> 138 us (0.920)
  Pallas kernels: 144 us -> 133 us
  local copies, waits for them, and re-layouts: 5.13 us -> 0 us
  other arithmetic: 0 us -> 3.58 us
    pallas_call x1, Pallas kernels: 144 us -> 133 us  [shards(): pl.pallas_call(functools.partial(kernel, nd, nz), out_shape=(jax.ShapeDty...]
    unnamed x2 -> x0, local copies, waits for them, and re-layouts: 3.74 us -> none
    convert_element_type x0 -> x2, other arithmetic: none -> 3.58 us  [shards(): return (grad_up.astype(F32), grad_down.astype(F32))]
where the time goes in v2:
time: 138 us
  Pallas kernels  133 us (96%)
  other arithmetic  3.58 us (3%)
    pallas_call x1, Pallas kernels, shards(): pl.pallas_call(functools.partial(kernel, nd, nz), out_shape=(jax.ShapeDty...  133 us
    convert_element_type x2, other arithmetic, shards(): return (grad_up.astype(F32), grad_down.astype(F32))  3.58 us

profile of v2, /device:TPU:8, one launch (start us, length us, event | category | flops | bytes accessed | tf_op | source)
XLA Modules:
  0.0 137.5 jit_solution(1912828176568089275)
XLA Ops:
  0.6 133.3 %shard_map.68 = (bf16[2,32,2048]{2,1,0:T(8,128)(2,1)}, bf16[2,128,512]{2,1,0:T(8,128)(2,1)}) custom-call(s32[1,128]{1,0:T(1,128)} %bitcast.1, bf16[1280,512]{1,0:T(8,128)(2,1)} %emb_hbm.1, bf16[2,512,2048]{2,1,0:T(8,128)(2,1)} %wu_hbm.1, bf16[2,2048,512]{2,1,0:T(8,128)(2,1)} %wd_hbm.1, bf16[128,512]{1,0:T(8,128)(2,1)} %cot.1), custom_call_target="tpu_custom_call" | custom-call | tf_op jit(solution)/shard_map/pallas_call | solution.py:612
  133.9 1.8 %convert_element_type.6 = f32[2,32,2048]{2,1,0:T(8,128)} convert(bf16[2,32,2048]{2,1,0:T(8,128)(2,1)} %get-tuple-element.4) | non-fusion elementwise | flops 131072 | bytes 786432 | tf_op jit(solution)/shard_map/convert_element_type | solution.py:625
  135.7 1.8 %convert_element_type.7 = f32[2,128,512]{2,1,0:T(8,128)} convert(bf16[2,128,512]{2,1,0:T(8,128)(2,1)} %get-tuple-element.5) | non-fusion elementwise | flops 131072 | bytes 786432 | tf_op jit(solution)/shard_map/convert_element_type | solution.py:625

commit v3 on v2

--- a/solution.py
+++ b/solution.py
@@ -38,10 +38,10 @@
     bsend, bpair, wsend, wbuf, zsend, zbuf,
     corr, unit, scales, slope,
     rbuf, wus, wds, norm_t, hid_t, slope_s,
-    gu, gd, gus, gds, gurecv, gdrecv, gx, gsum, csend, crecv,
+    gu, gd, gus, gds, gurecv, gdrecv, csend, crecv,
     load_sem, e_s, e_r, e2_s, e2_r, d_s, d_r, n_s, n_r,
     f_s, f_r, a_s, a_r, t_s, t_r, u_s, u_r, y_s, y_r,
-    b_s, b_r, w_s, w_r, z_s, z_r, ring_s, ring_r, g_s, g_r, h_s, h_r, x_s, x_r, c_s, c_r,
+    b_s, b_r, w_s, w_r, z_s, z_r, ring_s, ring_r, g_s, g_r, h_s, h_r, c_s, c_r,
 ):
     T, D = cot.shape
     L, _, FF = wu.shape
@@ -150,10 +150,17 @@
         t = (lane + i) % span
         return remote(all_n.at[t], all_n.at[t], n_s.at[i], n_r.at[t], depth=2 * (half * span + t))
 
+    def combine(first, second):
+        product = nn(first[...], second[...])
+        all_n[lane] = (product + first[...].astype(F32) + second[...].astype(F32)).astype(BF16)
+
+    @pl.when(core == 1)
+    def _():
+        combine(pair_d, own_d)
+
     @pl.when(core == 0)
     def _():
-        product = nn(own_d[...], pair_d[...])
-        all_n[lane] = (product + own_d[...].astype(F32) + pair_d[...].astype(F32)).astype(BF16)
+        combine(own_d, pair_d)
         each(1, span, lambda i: n_copy(i).start())
 
     def on(condition, f):
@@ -237,10 +244,35 @@
         return pl.ds(c * Q, Q)
 
     def u_copy(c):
-        return remote(usend.at[rows_of(c)], ubuf.at[lane], u_s.at[c], u_r.at[lane], depth=2 * (half * span + c))
-
-    def u_arrival(c):
-        return remote(usend.at[rows_of(c)], ubuf.at[c], u_s.at[c], u_r.at[c], depth=2 * (half * span + c))
+        return remote(usend.at[rows_of(c)], ubuf.at[core, lane], u_s.at[c], u_r.at[core, lane], depth=2 * (half * span + c))
+
+    def u_arrival(j, c):
+        return remote(usend.at[rows_of(c)], ubuf.at[j, c], u_s.at[c], u_r.at[j, c], depth=2 * (half * span + c))
+
+    def spread(src, dst, copy):
+        for c in range(span):
+            @pl.when((core == 1) | (lane != c))
+            def _(c=c):
+                copy(c).start()
+
+            @pl.when((core == 0) & (lane == c))
+            def _(c=c):
+                dst[0, c] = src[rows_of(c), :]
+
+    def collect(arrival):
+        for c in range(span):
+            arrival(1, c).wait_recv()
+
+            @pl.when(lane != c)
+            def _(c=c):
+                arrival(0, c).wait_recv()
+
+    def spread_sent(copy):
+        for c in range(span):
+            pl.when((core == 1) | (lane != c))(copy(c).wait_send)
+
+    def both_of(buf, c):
+        return buf[0, c].astype(F32) + buf[1, c].astype(F32)
 
     mine = pl.ds(pl.multiple_of(lane * Q, Q), Q)
 
@@ -275,11 +307,21 @@
 
     @pl.when(core == 0)
     def _():
+        usend[...] = times(change, all_n[lane]).astype(BF16)
+
+    @pl.when(core == 1)
+    def _():
+        usend[...] = times(change, own_d[...]).astype(BF16)
+
+    spread(usend, ubuf, u_copy)
+    pending.append(lambda: spread_sent(u_copy))
+
+    @pl.when(core == 0)
+    def _():
         tsend[...] = times(change, own_d[...]).astype(BF16)
         t_copy.start()
         each(1, span, lambda i: n_arrival(i).wait_recv())
-        for c in range(span):
-            u_arrival(c).wait_recv()
+        collect(u_arrival)
 
         @pl.when(half == 0)
         def _():
@@ -293,7 +335,7 @@
         for c in range(span):
             ysend[c] = y.astype(BF16)
             give(ysend, ybuf, y_s, y_r, c)
-            y = times(y, all_n[c]) + ubuf[c].astype(F32)
+            y = times(y, all_n[c]) + both_of(ubuf, c)
 
         @pl.when(half == 0)
         def _():
@@ -306,9 +348,6 @@
     @pl.when(core == 1)
     def _():
         t_copy.wait_recv()
-        usend[...] = times(change + tpair[...].astype(F32), own_d[...]).astype(BF16)
-        for c in range(span):
-            u_copy(c).start()
         take(ysend, ybuf, y_s, y_r)
         corr[...] = (
             cbuf[RELAX].astype(F32) + tpair[...].astype(F32) + times(ybuf[...].astype(F32), pair_d[...])
@@ -324,12 +363,7 @@
         given(ysend, ybuf, y_s, y_r)
         pl.when(half == 0)(c_copy.wait_send)
 
-    def u_sent():
-        for c in range(span):
-            u_copy(c).wait_send()
-
     on(core == 0, scan_sent)
-    on(core == 1, u_sent)
 
     steps = ((nz // 2, nz - 1 - nz // 2), (nz - 1 - nz // 2, nz // 2))
     most = nz // 2
@@ -376,10 +410,6 @@
     def gather_step(s):
         for layer in range(L):
             ring_step(layer, s)
-        for layer in range(L):
-            for way in range(2):
-                if s < steps[layer][way]:
-                    prepare(layer, ring_slot(way, s))
 
     v = corr[...]
     for layer in range(L):
@@ -401,9 +431,6 @@
         def _():
             a_copy(s).start()
 
-        if s == 0:
-            prepare(0, z)
-            prepare(1, z)
         if s < most:
             gather_step(s)
 
@@ -420,12 +447,23 @@
     b_copy = remote(bsend, bpair, b_s, b_r, depth=k + 1 - 2 * core)
 
     def w_copy(c):
-        return remote(wsend.at[rows_of(c)], wbuf.at[lane], w_s.at[c], w_r.at[lane], depth=2 * (half * span + c))
-
-    def w_arrival(c):
-        return remote(wsend.at[rows_of(c)], wbuf.at[c], w_s.at[c], w_r.at[c], depth=2 * (half * span + c))
+        return remote(wsend.at[rows_of(c)], wbuf.at[core, lane], w_s.at[c], w_r.at[core, lane], depth=2 * (half * span + c))
+
+    def w_arrival(j, c):
+        return remote(wsend.at[rows_of(c)], wbuf.at[j, c], w_s.at[c], w_r.at[j, c], depth=2 * (half * span + c))
 
     change = abuf[RELAX].astype(F32) - abuf[RELAX - 1].astype(F32)
+
+    @pl.when(core == 1)
+    def _():
+        wsend[...] = times_t(change, all_n[lane]).astype(BF16)
+
+    @pl.when(core == 0)
+    def _():
+        wsend[...] = times_t(change, own_d[...]).astype(BF16)
+
+    spread(wsend, wbuf, w_copy)
+    pending.append(lambda: spread_sent(w_copy))
 
     @pl.when(core == 1)
     def _():
@@ -437,21 +475,7 @@
 
     @pl.when(core == 0)
     def _():
-        b_copy.wait_recv()
-        wsend[...] = times_t(change + bpair[...].astype(F32), own_d[...]).astype(BF16)
-        for c in range(span):
-            @pl.when(lane != c)
-            def _(c=c):
-                w_copy(c).start()
-
-            @pl.when(lane == c)
-            def _(c=c):
-                wbuf[c] = wsend[rows_of(c), :]
-
-        for c in range(span):
-            @pl.when(lane != c)
-            def _(c=c):
-                w_arrival(c).wait_recv()
+        collect(w_arrival)
 
         @pl.when(half == 1)
         def _():
@@ -465,13 +489,22 @@
         for c in reversed(range(span)):
             zsend[c] = y.astype(BF16)
             give(zsend, zbuf, z_s, z_r, c)
-            y = times_t(y, all_n[c]) + wbuf[c].astype(F32)
+            y = times_t(y, all_n[c]) + both_of(wbuf, c)
 
         @pl.when(half == 1)
         def _():
             csend[1] = y.astype(BF16)
             c_back.start()
 
+    def prepare_slot(j):
+        for layer in range(L):
+            prepare(layer, j)
+
+    each(0, nz, prepare_slot)
+
+    @pl.when(core == 0)
+    def _():
+        b_copy.wait_recv()
         take(zsend, zbuf, z_s, z_r)
         corr[...] = (
             abuf[RELAX].astype(F32) + bpair[...].astype(F32) + times_t(zbuf[...].astype(F32), pair_d[...])
@@ -484,8 +517,6 @@
 
     def w_sent():
         given(zsend, zbuf, z_s, z_r)
-        for c in range(span):
-            pl.when(lane != c)(w_copy(c).wait_send)
         pl.when(half == 1)(c_back.wait_send)
 
     on(core == 0, w_sent)
@@ -507,42 +538,36 @@
         gu[layer] += nn(norm_t[layer, j], delta)
         gd[layer] += nn(hid_t[layer, j], low)
 
-    rows, part = D // ndp, D // 2
-    other = (1 - x) * nz + z
-
-    def x_copy(layer):
-        return remote(
-            gus.at[layer, pl.ds(pl.multiple_of((1 - x) * part, part), part)], gx.at[layer],
-            x_s.at[layer], x_r.at[layer], dp=other,
-        )
+    rows = D // ndp
 
     def h_copy(layer):
         return remote(
             gds.at[layer, pl.ds(pl.multiple_of((1 - x) * F, F), F)], gdrecv.at[layer],
-            h_s.at[layer], h_r.at[layer], dp=other,
+            h_s.at[layer], h_r.at[layer], dp=(1 - x) * nz + z,
         )
 
     def g_copy(layer, i):
-        t = (z + i) % nz
+        t = (p + i) % ndp
         return remote(
-            gsum.at[layer, pl.ds(pl.multiple_of(t * rows, rows), rows)], gurecv.at[layer, z],
-            g_s.at[layer, i], g_r.at[layer, z], dp=x * nz + t,
+            gus.at[layer, pl.ds(pl.multiple_of(t * rows, rows), rows)], gurecv.at[layer, p],
+            g_s.at[layer, i], g_r.at[layer, p], dp=t,
         )
 
     def g_arrival(layer, i):
-        t = (z + i) % nz
+        t = (p + i) % ndp
         return remote(
-            gsum.at[layer, pl.ds(pl.multiple_of(t * rows, rows), rows)], gurecv.at[layer, t],
-            g_s.at[layer, i], g_r.at[layer, t], dp=x * nz + t,
+            gus.at[layer, pl.ds(pl.multiple_of(t * rows, rows), rows)], gurecv.at[layer, t],
+            g_s.at[layer, i], g_r.at[layer, t], dp=t,
         )
 
-    def send_halves(layer):
-        gus[layer] = gu[layer].astype(BF16)
-        x_copy(layer).start()
+    def send_sums(layer):
         gds[layer] = gd[layer].astype(BF16)
         h_copy(layer).start()
-        pending.append(x_copy(layer).wait_send)
+        gus[layer] = gu[layer].astype(BF16)
+        each(1, ndp, lambda i: g_copy(layer, i).start())
+        gurecv[layer, p] = gus[layer, pl.ds(pl.multiple_of(p * rows, rows), rows), :]
         pending.append(h_copy(layer).wait_send)
+        pending.append(lambda: each(1, ndp, lambda i: g_copy(layer, i).wait_send()))
 
     contract(1, z)
     contract(0, z)
@@ -554,25 +579,18 @@
                 if s < steps[layer][way]:
                     contract(layer, ring_slot(way, s))
             if s == most - 1:
-                send_halves(layer)
-
-    for layer in (1, 0):
-        x_copy(layer).wait_recv()
-        gsum[layer] = (gu[layer, pl.ds(pl.multiple_of(x * part, part), part), :] + gx[layer].astype(F32)).astype(BF16)
-        each(1, nz, lambda i: g_copy(layer, i).start())
-        gurecv[layer, z] = gsum[layer, pl.ds(pl.multiple_of(z * rows, rows), rows), :]
-        pending.append(lambda layer=layer: each(1, nz, lambda i: g_copy(layer, i).wait_send()))
+                send_sums(layer)
 
     for layer in (1, 0):
         h_copy(layer).wait_recv()
         gd_out[layer] = (
             gd[layer, pl.ds(pl.multiple_of(x * F, F), F), :] + gdrecv[layer].astype(F32)
         ).astype(BF16)
-    for layer in (1, 0):
-        each(1, nz, lambda i: g_arrival(layer, i).wait_recv())
+        each(1, ndp, lambda i: g_arrival(layer, i).wait_recv())
         for j in range(nz):
-            gu_out[layer, :, j * F:(j + 1) * F] = gurecv[layer, j, :, :F]
-            gu_out[layer, :, FF // 2 + j * F:FF // 2 + (j + 1) * F] = gurecv[layer, j, :, F:]
+            both = (gurecv[layer, j].astype(F32) + gurecv[layer, nz + j].astype(F32)).astype(BF16)
+            gu_out[layer, :, j * F:(j + 1) * F] = both[:, :F]
+            gu_out[layer, :, FF // 2 + j * F:FF // 2 + (j + 1) * F] = both[:, F:]
 
     for wait in pending:
         wait()
@@ -592,20 +610,19 @@
         V((nd, R, D // 2), BF16), V((nd, R, D // 2), BF16), V((nd, R, D // 2), BF16),
         V((D, D), BF16), V((D, D), BF16), V((span, D, D), BF16),
         V((RELAX + 1, T, D), BF16), V((RELAX, T, D), BF16), V((RELAX + 1, T, D), BF16), V((RELAX, T, D), BF16),
-        V((T, D), BF16), V((T, D), BF16), V((T, D), BF16), V((span, Q, D), BF16), V((span, Q, D), BF16), V((T, D), BF16),
-        V((T, D), BF16), V((T, D), BF16), V((T, D), BF16), V((span, Q, D), BF16), V((span, Q, D), BF16), V((T, D), BF16),
+        V((T, D), BF16), V((T, D), BF16), V((T, D), BF16), V((2, span, Q, D), BF16), V((span, Q, D), BF16), V((T, D), BF16),
+        V((T, D), BF16), V((T, D), BF16), V((T, D), BF16), V((2, span, Q, D), BF16), V((span, Q, D), BF16), V((T, D), BF16),
         V((T, D), F32), V((L, T, D), F32), V((L, T, 1), F32), V((L, T, FF), F32),
         V((2 * L, nz, T, D), BF16), V((L, D, 2 * F), BF16), V((L, 2 * F, D), BF16),
         V((L, nz, D, T), BF16), V((L, nz, 2 * F, T), BF16), V((L, nz, T, 2 * F), F32),
         V((L, D, 2 * F), F32), V((L, 2 * F, D), F32), V((L, D, 2 * F), BF16), V((L, 2 * F, D), BF16),
-        V((L, nz, D // ndp, 2 * F), BF16), V((L, F, D), BF16), V((L, D // 2, 2 * F), BF16), V((L, D // 2, 2 * F), BF16),
+        V((L, ndp, D // ndp, 2 * F), BF16), V((L, F, D), BF16),
         V((2, Q, D), BF16), V((2, Q, D), BF16),
         sem((3,)), sem((nd,)), sem((nd,)), sem((nd,)), sem((nd,)), sem, sem, sem((nchip,)), sem((nchip,)),
         sem((RELAX,)), sem((RELAX,)), sem((RELAX,)), sem((RELAX,)),
-        sem, sem, sem((nchip,)), sem((nchip,)), sem((nchip, 2)), sem((nchip,)),
-        sem, sem, sem((nchip,)), sem((nchip,)), sem((nchip, 2)), sem((nchip,)),
-        sem((2 * L, 2, most)), sem((2 * L, 2, most)), sem((L, nz)), sem((L, nz)), sem((L,)), sem((L,)),
-        sem((L,)), sem((L,)), sem((2,)), sem((2,)),
+        sem, sem, sem((nchip,)), sem((2, nchip)), sem((nchip, 2)), sem((nchip,)),
+        sem, sem, sem((nchip,)), sem((2, nchip)), sem((nchip, 2)), sem((nchip,)),
+        sem((2 * L, 2, most)), sem((2 * L, 2, most)), sem((L, ndp)), sem((L, ndp)), sem((L,)), sem((L,)), sem((2,)), sem((2,)),
     ]
     vmem = pl.BlockSpec(memory_space=pltpu.VMEM)
     hbm = pl.BlockSpec(memory_space=pl.ANY)

time: 138 us -> 131 us (0.949)
  Pallas kernels: 133 us -> 126 us
    pallas_call x1, Pallas kernels: 133 us -> 126 us  [shards(): pl.pallas_call(functools.partial(kernel, nd, nz), out_shape=(jax.ShapeDty...]
where the time goes in v3:
time: 131 us
  Pallas kernels  126 us (96%)
  other arithmetic  3.58 us (3%)
    pallas_call x1, Pallas kernels, shards(): pl.pallas_call(functools.partial(kernel, nd, nz), out_shape=(jax.ShapeDty...  126 us
    convert_element_type x2, other arithmetic, shards(): return (grad_up.astype(F32), grad_down.astype(F32))  3.58 us

profile of v3, /device:TPU:8, one launch (start us, length us, event | category | flops | bytes accessed | tf_op | source)
XLA Modules:
  0.0 130.7 jit_solution(14054427948230765645)
XLA Ops:
  0.6 126.5 %shard_map.68 = (bf16[2,32,2048]{2,1,0:T(8,128)(2,1)}, bf16[2,128,512]{2,1,0:T(8,128)(2,1)}) custom-call(s32[1,128]{1,0:T(1,128)} %bitcast.1, bf16[1280,512]{1,0:T(8,128)(2,1)} %emb_hbm.1, bf16[2,512,2048]{2,1,0:T(8,128)(2,1)} %wu_hbm.1, bf16[2,2048,512]{2,1,0:T(8,128)(2,1)} %wd_hbm.1, bf16[128,512]{1,0:T(8,128)(2,1)} %cot.1), custom_call_target="tpu_custom_call" | custom-call | tf_op jit(solution)/shard_map/pallas_call | solution.py:629
  127.1 1.8 %convert_element_type.6 = f32[2,32,2048]{2,1,0:T(8,128)} convert(bf16[2,32,2048]{2,1,0:T(8,128)(2,1)} %get-tuple-element.4) | non-fusion elementwise | flops 131072 | bytes 786432 | tf_op jit(solution)/shard_map/convert_element_type | solution.py:642
  128.9 1.8 %convert_element_type.7 = f32[2,128,512]{2,1,0:T(8,128)} convert(bf16[2,128,512]{2,1,0:T(8,128)(2,1)} %get-tuple-element.5) | non-fusion elementwise | flops 131072 | bytes 786432 | tf_op jit(solution)/shard_map/convert_element_type | solution.py:642

commit v4 on v3

--- a/solution.py
+++ b/solution.py
@@ -127,10 +127,8 @@
         total = total + nn(wu[1, rows, :], wd[1])
         own_d[rows, :] = (GAMMA * total).astype(BF16)
 
-    each(0, D // 128, coarse_rows)
+    each(0, D // 256, coarse_rows)
     d_copy = remote(own_d, pair_d, d_s, d_r, depth=k + 1 - 2 * core)
-    d_copy.start()
-    pending.append(d_copy.wait_send)
 
     each(1, nd, lambda i: pick_arrival(i).wait_recv())
     total = erecv[0].astype(F32)
@@ -140,7 +138,9 @@
     each(1, nd, lambda i: start_copy(i).start())
     pending.append(lambda: each(1, nd, lambda i: start_copy(i).wait_send()))
 
-    d_copy.wait_recv()
+    each(D // 256, D // 128, coarse_rows)
+    d_copy.start()
+    pending.append(d_copy.wait_send)
 
     def n_copy(i):
         t = (lane + i) % span
@@ -154,25 +154,28 @@
         product = nn(first[...], second[...])
         all_n[lane] = (product + first[...].astype(F32) + second[...].astype(F32)).astype(BF16)
 
-    @pl.when(core == 1)
-    def _():
-        combine(pair_d, own_d)
-
-    @pl.when(core == 0)
-    def _():
-        combine(own_d, pair_d)
-        each(1, span, lambda i: n_copy(i).start())
+    def share():
+        d_copy.wait_recv()
+
+        @pl.when(core == 1)
+        def _():
+            combine(pair_d, own_d)
+
+        @pl.when(core == 0)
+        def _():
+            combine(own_d, pair_d)
+            each(1, span, lambda i: n_copy(i).start())
+
+        for piece in range(2):
+            at = pl.multiple_of(piece * (FF // 2) + z * F, 128)
+            for layer in range(L):
+                wus[layer, :, piece * F:(piece + 1) * F] = wu[layer, :, pl.ds(at, F)]
+                wds[layer, piece * F:(piece + 1) * F, :] = wd[layer, pl.ds(at, F), :]
 
     def on(condition, f):
         pending.append(lambda: pl.when(condition)(f))
 
     on(core == 0, lambda: each(1, span, lambda i: n_copy(i).wait_send()))
-
-    for piece in range(2):
-        at = pl.multiple_of(piece * (FF // 2) + z * F, 128)
-        for layer in range(L):
-            wus[layer, :, piece * F:(piece + 1) * F] = wu[layer, :, pl.ds(at, F)]
-            wds[layer, piece * F:(piece + 1) * F, :] = wd[layer, pl.ds(at, F), :]
 
     each(1, nd, lambda i: start_arrival(i).wait_recv())
     for c in range(nd):
@@ -221,6 +224,8 @@
         def _():
             f_copy(s).start()
 
+        pl.when(s == 0)(share)
+
         @pl.when(k > 0)
         def _():
             f_copy(s).wait_recv()
@@ -571,14 +576,15 @@
 
     contract(1, z)
     contract(0, z)
-    for s in range(most):
-        for layer in (1, 0):
-            ring_step(L + layer, s)
-        for layer in (1, 0):
+    for s in range(most + 1):
+        turns = [(layer, at) for layer, at in ((1, s), (0, s - 1)) if 0 <= at < most]
+        for layer, at in turns:
+            ring_step(L + layer, at)
+        for layer, at in turns:
             for way in range(2):
-                if s < steps[layer][way]:
-                    contract(layer, ring_slot(way, s))
-            if s == most - 1:
+                if at < steps[layer][way]:
+                    contract(layer, ring_slot(way, at))
+            if at == most - 1:
                 send_sums(layer)
 
     for layer in (1, 0):
@@ -594,6 +600,11 @@
 
     for wait in pending:
         wait()
+
+
+def widen(up, down, up_out, down_out):
+    up_out[...] = up[...].astype(F32)
+    down_out[...] = down[...].astype(F32)
 
 
 def shards(nd, ndp, token_ids, embedding, w_up, w_down, cotangent):
@@ -639,7 +650,15 @@
             collective_id=0, has_side_effects=True, vmem_limit_bytes=58 * 1024 * 1024
         ),
     )(token_ids[None, :], embedding, w_up, w_down, cotangent)
-    return grad_up.astype(F32), grad_down.astype(F32)
+    return pl.pallas_call(
+        widen,
+        out_shape=(
+            jax.ShapeDtypeStruct(grad_up.shape, F32),
+            jax.ShapeDtypeStruct(grad_down.shape, F32),
+        ),
+        in_specs=[vmem, vmem],
+        out_specs=(vmem, vmem),
+    )(grad_up, grad_down)
 
 
 def solution(mesh):

time: 131 us -> 134 us (1.023)
  Pallas kernels: 126 us -> 132 us
  other arithmetic: 3.58 us -> 0 us
    convert_element_type x2 -> x0, other arithmetic: 3.58 us -> none  [shards(): return (grad_up.astype(F32), grad_down.astype(F32))]
    pallas_call x1, Pallas kernels: 126 us -> 130 us  [shards(): pl.pallas_call(functools.partial(kernel, nd, nz), out_shape=(jax.ShapeDty...]
    pallas_call x0 -> x1, Pallas kernels: none -> 2.03 us  [shards(): pl.pallas_call(widen, out_shape=(jax.ShapeDtypeStruct(grad_up.shape, F32)...]
where the time goes in v4:
time: 134 us; the launch traced here: 133 us
  Pallas kernels  132 us (99%)
    pallas_call x1, Pallas kernels, shards(): pl.pallas_call(functools.partial(kernel, nd, nz), out_shape=(jax.ShapeDty...  130 us

profile of v4, /device:TPU:8, one launch (start us, length us, event | category | flops | bytes accessed | tf_op | source)
XLA Modules:
  0.0 132.6 jit_solution(2448056607051334025)
XLA Ops:
  0.6 129.9 %shard_map.68 = (bf16[2,32,2048]{2,1,0:T(8,128)(2,1)}, bf16[2,128,512]{2,1,0:T(8,128)(2,1)}) custom-call(s32[1,128]{1,0:T(1,128)} %bitcast.1, bf16[1280,512]{1,0:T(8,128)(2,1)} %emb_hbm.1, bf16[2,512,2048]{2,1,0:T(8,128)(2,1)} %wu_hbm.1, bf16[2,2048,512]{2,1,0:T(8,128)(2,1)} %wd_hbm.1, bf16[128,512]{1,0:T(8,128)(2,1)} %cot.1), custom_call_target="tpu_custom_call" | custom-call | tf_op jit(solution)/shard_map/pallas_call | solution.py:640
  130.5 2.0 %shard_map.69 = (f32[2,32,2048]{2,1,0:T(8,128)}, f32[2,128,512]{2,1,0:T(8,128)}) custom-call(bf16[2,32,2048]{2,1,0:T(8,128)(2,1)} %get-tuple-element.4.up, bf16[2,128,512]{2,1,0:T(8,128)(2,1)} %get-tuple-element.5.down), custom_call_target="tpu_custom_call" | custom-call | tf_op jit(solution)/shard_map/pallas_call | solution.py:653

commit v5 on v3

--- a/solution.py
+++ b/solution.py
@@ -571,14 +571,15 @@
 
     contract(1, z)
     contract(0, z)
-    for s in range(most):
-        for layer in (1, 0):
-            ring_step(L + layer, s)
-        for layer in (1, 0):
+    for s in range(most + 1):
+        turns = [(layer, at) for layer, at in ((1, s), (0, s - 1)) if 0 <= at < most]
+        for layer, at in turns:
+            ring_step(L + layer, at)
+        for layer, at in turns:
             for way in range(2):
-                if s < steps[layer][way]:
-                    contract(layer, ring_slot(way, s))
-            if s == most - 1:
+                if at < steps[layer][way]:
+                    contract(layer, ring_slot(way, at))
+            if at == most - 1:
                 send_sums(layer)
 
     for layer in (1, 0):
@@ -594,6 +595,11 @@
 
     for wait in pending:
         wait()
+
+
+def widen(up, down, up_out, down_out):
+    up_out[...] = up[...].astype(F32)
+    down_out[...] = down[...].astype(F32)
 
 
 def shards(nd, ndp, token_ids, embedding, w_up, w_down, cotangent):
@@ -639,7 +645,15 @@
             collective_id=0, has_side_effects=True, vmem_limit_bytes=58 * 1024 * 1024
         ),
     )(token_ids[None, :], embedding, w_up, w_down, cotangent)
-    return grad_up.astype(F32), grad_down.astype(F32)
+    return pl.pallas_call(
+        widen,
+        out_shape=(
+            jax.ShapeDtypeStruct(grad_up.shape, F32),
+            jax.ShapeDtypeStruct(grad_down.shape, F32),
+        ),
+        in_specs=[vmem, vmem],
+        out_specs=(vmem, vmem),
+    )(grad_up, grad_down)
 
 
 def solution(mesh):

time: 131 us -> 131 us (level)
  Pallas kernels: 126 us -> 130 us
  other arithmetic: 3.58 us -> 0 us
    convert_element_type x2 -> x0, other arithmetic: 3.58 us -> none  [shards(): return (grad_up.astype(F32), grad_down.astype(F32))]
    pallas_call x0 -> x1, Pallas kernels: none -> 2.03 us  [shards(): pl.pallas_call(widen, out_shape=(jax.ShapeDtypeStruct(grad_up.shape, F32)...]
    pallas_call x1, Pallas kernels: 126 us -> 128 us  [shards(): pl.pallas_call(functools.partial(kernel, nd, nz), out_shape=(jax.ShapeDty...]
where the time goes in v5:
time: 131 us
  Pallas kernels  130 us (99%)
    pallas_call x1, Pallas kernels, shards(): pl.pallas_call(functools.partial(kernel, nd, nz), out_shape=(jax.ShapeDty...  128 us

profile of v5, /device:TPU:8, one launch (start us, length us, event | category | flops | bytes accessed | tf_op | source)
XLA Modules:
  0.0 130.6 jit_solution(13559862923015524412)
XLA Ops:
  0.6 127.9 %shard_map.68 = (bf16[2,32,2048]{2,1,0:T(8,128)(2,1)}, bf16[2,128,512]{2,1,0:T(8,128)(2,1)}) custom-call(s32[1,128]{1,0:T(1,128)} %bitcast.1, bf16[1280,512]{1,0:T(8,128)(2,1)} %emb_hbm.1, bf16[2,512,2048]{2,1,0:T(8,128)(2,1)} %wu_hbm.1, bf16[2,2048,512]{2,1,0:T(8,128)(2,1)} %wd_hbm.1, bf16[128,512]{1,0:T(8,128)(2,1)} %cot.1), custom_call_target="tpu_custom_call" | custom-call | tf_op jit(solution)/shard_map/pallas_call | solution.py:635
  128.5 2.0 %shard_map.69 = (f32[2,32,2048]{2,1,0:T(8,128)}, f32[2,128,512]{2,1,0:T(8,128)}) custom-call(bf16[2,32,2048]{2,1,0:T(8,128)(2,1)} %get-tuple-element.4.up, bf16[2,128,512]{2,1,0:T(8,128)(2,1)} %get-tuple-element.5.down), custom_call_target="tpu_custom_call" | custom-call | tf_op jit(solution)/shard_map/pallas_call | solution.py:648

commit v6 on v3

--- a/solution.py
+++ b/solution.py
@@ -594,6 +594,11 @@
 
     for wait in pending:
         wait()
+
+
+def widen(up, down, up_out, down_out):
+    up_out[...] = up[...].astype(F32)
+    down_out[...] = down[...].astype(F32)
 
 
 def shards(nd, ndp, token_ids, embedding, w_up, w_down, cotangent):
@@ -639,7 +644,15 @@
             collective_id=0, has_side_effects=True, vmem_limit_bytes=58 * 1024 * 1024
         ),
     )(token_ids[None, :], embedding, w_up, w_down, cotangent)
-    return grad_up.astype(F32), grad_down.astype(F32)
+    return pl.pallas_call(
+        widen,
+        out_shape=(
+            jax.ShapeDtypeStruct(grad_up.shape, F32),
+            jax.ShapeDtypeStruct(grad_down.shape, F32),
+        ),
+        in_specs=[vmem, vmem],
+        out_specs=(vmem, vmem),
+    )(grad_up, grad_down)
 
 
 def solution(mesh):

time: 131 us -> 129 us (0.985)
  other arithmetic: 3.58 us -> 0 us
  Pallas kernels: 126 us -> 129 us
    convert_element_type x2 -> x0, other arithmetic: 3.58 us -> none  [shards(): return (grad_up.astype(F32), grad_down.astype(F32))]
    pallas_call x0 -> x1, Pallas kernels: none -> 2.03 us  [shards(): pl.pallas_call(widen, out_shape=(jax.ShapeDtypeStruct(grad_up.shape, F32)...]
where the time goes in v6:
time: 129 us
  Pallas kernels  129 us (100%)
    pallas_call x1, Pallas kernels, shards(): pl.pallas_call(functools.partial(kernel, nd, nz), out_shape=(jax.ShapeDty...  126 us

profile of v6, /device:TPU:8, one launch (start us, length us, event | category | flops | bytes accessed | tf_op | source)
XLA Modules:
  0.0 129.1 jit_solution(8881474444258887785)
XLA Ops:
  0.6 126.5 %shard_map.68 = (bf16[2,32,2048]{2,1,0:T(8,128)(2,1)}, bf16[2,128,512]{2,1,0:T(8,128)(2,1)}) custom-call(s32[1,128]{1,0:T(1,128)} %bitcast.1, bf16[1280,512]{1,0:T(8,128)(2,1)} %emb_hbm.1, bf16[2,512,2048]{2,1,0:T(8,128)(2,1)} %wu_hbm.1, bf16[2,2048,512]{2,1,0:T(8,128)(2,1)} %wd_hbm.1, bf16[128,512]{1,0:T(8,128)(2,1)} %cot.1), custom_call_target="tpu_custom_call" | custom-call | tf_op jit(solution)/shard_map/pallas_call | solution.py:634
  127.1 2.0 %shard_map.69 = (f32[2,32,2048]{2,1,0:T(8,128)}, f32[2,128,512]{2,1,0:T(8,128)}) custom-call(bf16[2,32,2048]{2,1,0:T(8,128)(2,1)} %get-tuple-element.4.up, bf16[2,128,512]{2,1,0:T(8,128)(2,1)} %get-tuple-element.5.down), custom_call_target="tpu_custom_call" | custom-call | tf_op jit(solution)/shard_map/pallas_call | solution.py:647
